TPU v7x, 32 devices: a whole 2x2x4 slice. The times are simulated.
32 devices in a mesh: groups: 2 (over y), inst: 4 (over z), tp: 4 (over x, core).
Axes of the slice: x: 2, y: 2, z: 4, core: 2. Of those that a mesh axis runs over, the one named last changes fastest.
Arguments:
- tokens: bfloat16 [4, 2048, 8192], P(None, ('groups', 'inst'), 'tp'), parts along dimension 1, may hold values from -6 to 6
- key_value_weight: bfloat16 [8192, 2048], P('tp'), may hold values from -0.0625 to 0.0625
- adapter_down_weight: bfloat16 [64, 8192, 256], P(('groups', 'inst'), 'tp'), parts along dimension 0, may hold values from -0.0625 to 0.0625
- adapter_up_weight: bfloat16 [64, 2, 128, 1024], P(('groups', 'inst'), None, None, 'tp'), parts along dimension 0, may hold values from -0.5 to 0.5
- row_adapter_index: int32 [4, 2048], P(None, ('groups', 'inst')), parts along dimension 1, may hold values from 0 to 31, as said below
- ranks: int32 [64], P(('groups', 'inst')), parts along dimension 0, may hold values from 16 to 128, as said below
Outputs:
- kv_out: bfloat16 [4, 2048, 2, 1024], P(None, ('groups', 'inst'), None, 'tp'), parts along dimension 1
There are 2 independent parts, one for each index of `groups`. A program takes and returns all parts, laid end to end along the dimension named above; an argument that names none is the same for every part. Nothing has to cross between parts.
Inputs may be any that keep to these rules, and one draw needn't show every extreme that they name: `row_adapter_index`: adapter a is held by instance a // 8. In each step the 256 rows of one instance name adapters of one holder at most 128 times, and of some holder exactly 128 times. `ranks`: multiples of 16.
All inputs are finite; a program needn't handle non-finite values.
Results may differ from a plain program's by a relative error of at most 0.014.
Values may be sent and summed in bfloat16 or wider, within the bound.
No kernel may reach another device: no remote copies, remote signals or barrier semaphores. Data moves between devices by JAX's collectives and lax.ppermute only.
A program may use at most 128 MiB of HBM per device.

v0:
```python
import jax
import jax.numpy as jnp
from jax import lax
from jax.experimental import pallas as pl
from jax.experimental.pallas import tpu as pltpu
from jax.sharding import PartitionSpec as P

VMEM = 48 * 1024 * 1024
SMALL = pl.CostEstimate(flops=1024, bytes_accessed=1024, transcendentals=0)


def gather_kernel(starts, target_ref, x_ref, *outs):
    target = target_ref[...]
    for start, out in zip(starts, outs):
        slot = start + lax.broadcasted_iota(jnp.int32, (out.shape[0], 1), 0)
        sel = jnp.where(slot == target, 1.0, 0.0).astype(jnp.bfloat16)
        out[...] = jnp.dot(sel, x_ref[...], preferred_element_type=jnp.float32).astype(out.dtype)


def gather(starts, sizes, target, x):
    rows, width = x.shape
    tile = min(512, width)
    return pl.pallas_call(
        lambda *refs: gather_kernel(starts, *refs),
        out_shape=[jax.ShapeDtypeStruct((n, width), x.dtype) for n in sizes],
        grid=(width // tile,),
        in_specs=[
            pl.BlockSpec((1, rows), lambda c: (0, 0)),
            pl.BlockSpec((rows, tile), lambda c: (0, c)),
        ],
        out_specs=[pl.BlockSpec((n, tile), lambda c: (0, c)) for n in sizes],
        compiler_params=pltpu.CompilerParams(vmem_limit_bytes=VMEM),
        cost_estimate=SMALL,
        name="gather",
    )(target, x)


def spans(sizes):
    ends = [sum(sizes[: n + 1]) for n in range(len(sizes))]
    return [(end - size, end) for end, size in zip(ends, sizes)]


def down_kernel(count, ranks_ref, id_ref, *refs):
    xs, weight_ref, out_ref, total_ref = refs[:count], refs[count], refs[count + 1], refs[count + 2]
    adapter = pl.program_id(0)

    @pl.when(adapter == 0)
    def _():
        total_ref[...] = jnp.zeros_like(total_ref)

    for x_ref, (low, high) in zip(xs, spans([x.shape[0] for x in xs])):
        part = jnp.dot(x_ref[...], weight_ref[0], preferred_element_type=jnp.float32)
        column = lax.broadcasted_iota(jnp.int32, part.shape, 1) % (part.shape[1] // 2)
        keep = (id_ref[low:high] == adapter) & (column < ranks_ref[adapter])
        total_ref[low:high] += jnp.where(keep, part, 0.0)

    @pl.when(adapter == pl.num_programs(0) - 1)
    def _():
        out_ref[...] = total_ref[...].astype(out_ref.dtype)


def down(xs, ids, weight, ranks):
    adapters, width, rank2 = weight.shape
    rows = ids.shape[0]
    fixed = lambda a: (0, 0)
    return pl.pallas_call(
        lambda *refs: down_kernel(len(xs), *refs),
        out_shape=jax.ShapeDtypeStruct((rows, rank2), jnp.bfloat16),
        grid=(adapters,),
        in_specs=[pl.BlockSpec(memory_space=pltpu.SMEM), pl.BlockSpec((rows, 1), fixed)]
        + [pl.BlockSpec(x.shape, fixed) for x in xs]
        + [pl.BlockSpec((1, width, rank2), lambda a: (a, 0, 0))],
        out_specs=pl.BlockSpec((rows, rank2), fixed),
        scratch_shapes=[pltpu.VMEM((rows, rank2), jnp.float32)],
        compiler_params=pltpu.CompilerParams(vmem_limit_bytes=VMEM),
        cost_estimate=SMALL,
        name="down",
    )(ranks, ids, *xs, weight)


def up_kernel(count, id_ref, *refs):
    parts, weight_ref, outs = refs[:count], refs[count], refs[count + 1 :]
    adapters, halves, rank, columns = weight_ref.shape
    for out, (low, high) in zip(outs, spans([out.shape[0] for out in outs])):
        terms = [p[low:high] if len(p.shape) == 2 else p[n, low:high] for p in parts for n in range(p.shape[0] if len(p.shape) == 3 else 1)]
        total = terms[0].astype(jnp.float32)
        for term in terms[1:]:
            total = total + term.astype(jnp.float32)
        own = id_ref[low:high]
        for half in range(halves):
            shrink = total[:, half * rank : (half + 1) * rank]
            spread = jnp.concatenate(
                [jnp.where(own == a, shrink, 0.0).astype(jnp.bfloat16) for a in range(adapters)],
                axis=1,
            )
            matrix = weight_ref[:, half].reshape(adapters * rank, columns)
            out[:, half * columns : (half + 1) * columns] = jnp.dot(
                spread, matrix, preferred_element_type=jnp.float32
            ).astype(out.dtype)


def up(parts, ids, sizes, weight):
    _, halves, _, columns = weight.shape
    whole = pl.BlockSpec(memory_space=pltpu.VMEM)
    return pl.pallas_call(
        lambda *refs: up_kernel(len(parts), *refs),
        out_shape=[jax.ShapeDtypeStruct((n, halves * columns), jnp.bfloat16) for n in sizes],
        in_specs=[whole] * (2 + len(parts)),
        out_specs=[whole] * len(sizes),
        compiler_params=pltpu.CompilerParams(vmem_limit_bytes=VMEM),
        cost_estimate=SMALL,
        name="up",
    )(ids, *parts, weight)


def base_kernel(order_ref, x_ref, weight_ref, *outs):
    part = jnp.dot(x_ref[...], weight_ref[...], preferred_element_type=jnp.float32)
    if len(outs) == 1:
        outs[0][0] = part.astype(outs[0].dtype)
    else:
        share = pl.num_programs(0) // len(outs)
        for n, out in enumerate(outs):

            @pl.when(pl.program_id(0) // share == n)
            def _():
                out[0] = part.astype(out.dtype)


def base_blocks(x, weight, order, outputs, halves, columns, piece=0, pieces=1):
    rows, width = x.shape[0] // pieces, x.shape[1]
    blocks = order.shape[0]
    share = blocks // outputs

    def place(n):
        return lambda b, k, o: (
            jnp.clip(b - n * share, 0, share - 1),
            0,
            jnp.where(b < n * share, 0, jnp.where(b >= (n + 1) * share, halves - 1, k)),
        )

    return pl.pallas_call(
        base_kernel,
        out_shape=[jax.ShapeDtypeStruct((share, rows, halves * columns), jnp.bfloat16)] * outputs,
        grid_spec=pltpu.PrefetchScalarGridSpec(
            num_scalar_prefetch=1,
            grid=(blocks, halves),
            in_specs=[
                pl.BlockSpec((rows, width), lambda b, k, o: (piece, 0)),
                pl.BlockSpec((width, columns), lambda b, k, o: (0, k * blocks + o[b])),
            ],
            out_specs=[pl.BlockSpec((1, rows, columns), place(n)) for n in range(outputs)],
        ),
        compiler_params=pltpu.CompilerParams(vmem_limit_bytes=VMEM),
        cost_estimate=SMALL,
        name="base",
    )(order, x, weight)


def finish_kernel(starts, total_ref, target_ref, *refs):
    target, out_ref = target_ref[...], refs[-1]
    total = total_ref[...]
    for start, list_ref in zip(starts, refs):
        slot = start + lax.broadcasted_iota(jnp.int32, (1, list_ref.shape[0]), 1)
        sel = jnp.where(target == slot, 1.0, 0.0).astype(jnp.bfloat16)
        total = total + jnp.dot(sel, list_ref[...], preferred_element_type=jnp.float32)
    out_ref[...] = total.astype(out_ref.dtype)


def finish(total, target, starts, lists):
    rows, columns = total.shape
    tile = rows // 4
    return pl.pallas_call(
        lambda *refs: finish_kernel(starts, *refs),
        out_shape=jax.ShapeDtypeStruct((rows, columns), jnp.bfloat16),
        grid=(rows // tile,),
        in_specs=[
            pl.BlockSpec((tile, columns), lambda r: (r, 0)),
            pl.BlockSpec((tile, 1), lambda r: (r, 0)),
        ]
        + [pl.BlockSpec(part.shape, lambda r: (0, 0)) for part in lists],
        out_specs=pl.BlockSpec((tile, columns), lambda r: (r, 0)),
        compiler_params=pltpu.CompilerParams(vmem_limit_bytes=VMEM),
        cost_estimate=SMALL,
        name="finish",
    )(total, target, *lists)


def swap(x, axis, distance):
    count = lax.axis_size(axis)
    return lax.ppermute(x, axis, [(i, i ^ distance) for i in range(count)])


def together(*values):
    return lax.optimization_barrier(values)


def local(tokens, key_value_weight, adapter_down_weight, adapter_up_weight, row_adapter_index, ranks):
    steps, step_rows, width = tokens.shape
    inst_count = lax.axis_size("inst")
    tp_count = lax.axis_size("tp")
    held, _, rank2 = adapter_down_weight.shape
    halves, columns = adapter_up_weight.shape[1], adapter_up_weight.shape[3]
    rows = steps * step_rows
    me = lax.axis_index("inst")
    tp_me = lax.axis_index("tp")
    x = tokens.reshape(rows, width)
    ids = row_adapter_index.reshape(1, rows)
    chunk = 64
    pooled = inst_count == 4
    if pooled:
        own_cap, near_cap, far_cap, flex_cap = rows // 2, 448 * rows // 1024, 224 * rows // 1024, 288 * rows // 1024
    else:
        own_cap = near_cap = far_cap = flex_cap = 0
    holder = ids // held
    base_near = own_cap
    base_far2 = base_near + near_cap
    base_flex = base_far2 + far_cap
    base_far3 = base_flex + flex_cap
    base_over = base_far3 + far_cap
    if pooled:
        cls = holder ^ me
        hit = (cls == jnp.arange(4)[:, None]).astype(jnp.bfloat16)
        earlier = (jnp.arange(rows)[:, None] < jnp.arange(rows)[None, :]).astype(jnp.bfloat16)
        before = jnp.dot(hit, earlier, preferred_element_type=jnp.float32).astype(jnp.int32)
        counts = jnp.sum(hit.astype(jnp.int32), axis=1)
        place = jnp.sum(jnp.where(hit > 0, before, 0), axis=0, keepdims=True)
        over_near = jnp.maximum(counts[1] - near_cap, 0)
        extra2 = jnp.maximum(counts[2] - far_cap, 0)
        extra3 = jnp.maximum(counts[3] - far_cap, 0)
        over_far = jnp.maximum(extra2 + extra3 - flex_cap, 0)
        flex = place - far_cap + jnp.where(cls == 3, extra2, 0)
        far_target = jnp.where(
            place < far_cap,
            place + jnp.where(cls == 2, base_far2, base_far3),
            jnp.where(flex < flex_cap, flex + base_flex, flex - flex_cap + over_near + base_over),
        )
        near_target = jnp.where(
            place < near_cap, place + base_near, place - near_cap + base_over
        )
        target = jnp.where(cls == 0, place, jnp.where(cls == 1, near_target, far_target))
        over = over_near + over_far
    else:
        target = jnp.arange(rows)[None, :]
        over = jnp.int32(rows)
    target_column = target.reshape(rows, 1)
    ids_column = ids.reshape(rows, 1)

    def slot_ids(start, size):
        sel = target_column == (start + jnp.arange(size))[None, :]
        return jnp.sum(jnp.where(sel, ids_column + 1, 0), axis=0, keepdims=True) - 1

    def put(start, rows_back):
        sel = target_column == (start + jnp.arange(rows_back.shape[0]))[None, :]
        return jnp.dot(
            sel.astype(jnp.bfloat16), rows_back, preferred_element_type=jnp.float32
        )

    def held_ids(global_ids):
        local_ids = global_ids.reshape(-1, 1) - me * held
        return jnp.where((local_ids >= 0) & (local_ids < held), local_ids, -1)

    def add(a, b):
        return (a.astype(jnp.float32) + b.astype(jnp.float32)).astype(jnp.bfloat16)

    def gathered(part):
        return lax.all_gather(part, "tp", axis=0, tiled=False)

    def exchange(part):
        if tp_count != 4:
            return [lax.psum(part.astype(jnp.float32), "tp")]
        pair = add(part, swap(part, "tp", 1))
        return [pair, swap(pair, "tp", 2)]

    def shrink(xs, list_ids):
        return down(xs, list_ids, adapter_down_weight, ranks)

    def expand(parts, list_ids, sizes):
        return up(parts, list_ids, sizes, adapter_up_weight)

    def base_parts(x):
        order = jnp.arange(tp_count, dtype=jnp.int32)
        (part,) = base_blocks(x, key_value_weight, order, 1, halves, columns)
        return part

    def base_sent(part):
        return lax.all_to_all(part, "tp", 0, 0, tiled=True)

    def largest(value, axis):
        count = lax.axis_size(axis)
        most = value
        for d in range(1, count):
            most = jnp.maximum(
                most, lax.ppermute(value, axis, [(i, (i + d) % count) for i in range(count)])
            )
        return most

    def add_overflow(total, trips):
        def more(carry):
            return carry[0] < trips

        def one(carry):
            trip, total = carry
            start = base_over + trip * chunk
            (mine,) = gather([0], [chunk], target - start, x)
            x_all = lax.all_gather(mine, "inst", axis=0, tiled=True)
            ids_all = held_ids(lax.all_gather(slot_ids(start, chunk), "inst", axis=0, tiled=True))
            part = exchange(shrink([x_all], ids_all))
            (delta,) = expand(part, ids_all, [inst_count * chunk])
            back = lax.all_to_all(
                delta.reshape(inst_count, chunk, halves * columns), "inst", 0, 0, tiled=True
            )
            mine = jnp.sum(back.astype(jnp.float32), axis=0).astype(jnp.bfloat16)
            return trip + 1, total + put(start, mine)

        return lax.while_loop(more, one, (jnp.int32(0), total))[1]

    if not pooled:
        trips = (largest(largest(over, "inst"), "groups") + chunk - 1) // chunk
        total = add_overflow(
            jnp.sum(base_sent(base_parts(x)).astype(jnp.float32), axis=0), trips
        )
        return total.astype(jnp.bfloat16).reshape(steps, step_rows, halves, columns)

    all_ids = slot_ids(0, base_over)
    over = jnp.full((1, 1), over, jnp.int32)
    got1 = swap(jnp.concatenate([all_ids[:, base_near:base_far2], over], axis=1), "inst", 1)
    got2 = swap(jnp.concatenate([all_ids[:, base_far2:base_far3], over], axis=1), "inst", 2)
    got3 = swap(jnp.concatenate([all_ids[:, base_flex:base_over], over], axis=1), "inst", 3)

    target, got1, got2, got3 = together(target, got1, got2, got3)
    (g_flex,) = gather([base_flex], [flex_cap], target, x)
    r_flex = swap(g_flex, "inst", 2)
    x, target, _ = together(x, target, g_flex)
    (g_near,) = gather([base_near], [near_cap], target, x)
    r_near = swap(g_near, "inst", 1)
    most = jnp.max(jnp.concatenate([over] + [g[:, -1:] for g in (got1, got2, got3)], axis=1))
    trips = (largest(most, "groups") + chunk - 1) // chunk
    k_1, k_2, k_3 = held_ids(got1[:, :-1]), held_ids(got2[:, :-1]), held_ids(got3[:, :-1])
    k_2, k_flex = k_2[:far_cap], k_2[far_cap:]
    k_on, k_3 = k_3[:flex_cap], k_3[flex_cap:]
    k_own = held_ids(all_ids[:, :own_cap])
    k_on_2 = jnp.concatenate([k_on, k_2], axis=0)

    x, target, _ = together(x, target, g_near)
    g_3, g_own, g_2 = gather(
        [base_far3, 0, base_far2], [far_cap, own_cap, far_cap], target, x
    )
    x, g_own = together(x, g_own)
    part = base_parts(x)
    sent = base_sent(part)

    r_flex, g_3, g_2, trips, k_flex, k_own, k_on_2, k_on, k_3, k_1, k_2, _ = together(
        r_flex, g_3, g_2, trips, k_flex, k_own, k_on_2, k_on, k_3, k_1, k_2, part
    )
    r_3 = swap(g_3, "inst", 3)
    r_on = swap(r_flex, "inst", 1)
    s_flex = shrink([r_flex], k_flex)
    g_own, s_flex = together(g_own, s_flex)
    s_own = shrink([g_own], k_own)
    (d_flex,) = expand([gathered(s_flex)], k_flex, [flex_cap])

    r_3, g_2, s_own, d_flex = together(r_3, g_2, s_own, d_flex)
    r_2 = swap(g_2, "inst", 2)
    s_3 = shrink([r_3], k_3)
    (d_3,) = expand([gathered(s_3)], k_3, [far_cap])
    b_3 = swap(d_3, "inst", 3)

    r_near, d_3 = together(r_near, d_3)
    s_near = shrink([r_near], k_1)
    (d_near,) = expand([gathered(s_near)], k_1, [near_cap])
    b_near = swap(d_near, "inst", 1)

    r_on, r_2, d_near = together(r_on, r_2, d_near)
    s_on_2 = shrink([r_on, r_2], k_on_2)
    s_on, s_2 = s_on_2[:flex_cap], s_on_2[flex_cap:]
    (d_on,) = expand([gathered(s_on)], k_on, [flex_cap])
    b_on = swap(d_on, "inst", 1)
    s_2, d_on, b_3, b_near, sent = together(s_2, d_on, b_3, b_near, sent)
    (d_2,) = expand([gathered(s_2)], k_2, [far_cap])
    b_2 = swap(d_2, "inst", 2)
    b_on, d_2 = together(b_on, d_2)
    back_flex = d_flex + b_on
    b_flex = swap(back_flex, "inst", 2)
    s_own, sent, b_3, b_near, _ = together(s_own, sent, b_3, b_near, back_flex)
    (d_own,) = expand([gathered(s_own)], k_own, [own_cap])
    base = jnp.sum(sent.astype(jnp.float32), axis=0)
    total = add_overflow(base + put(0, jnp.concatenate([d_own, b_near], axis=0)), trips)
    total = total + put(base_far3, b_3)
    total = finish(total, target_column, [base_far2, base_flex], [b_2, b_flex])
    return total.reshape(steps, step_rows, halves, columns)


def solution(mesh):
    placed = (
        P(None, ("groups", "inst"), "tp"),
        P("tp", None),
        P(("groups", "inst"), "tp", None),
        P(("groups", "inst"), None, None, "tp"),
        P(None, ("groups", "inst")),
        P(("groups", "inst")),
    )
    return jax.shard_map(
        local,
        mesh=mesh,
        in_specs=placed,
        out_specs=P(None, ("groups", "inst"), None, "tp"),
        check_vma=False,
    )
```

profile of v0, /device:TPU:0, one launch (start us, length us, event | category | flops | bytes accessed | tf_op | source)
XLA Modules:
  0.0 228.1 jit_solution(12546402784128345753)
XLA Ops:
  6.5 0.7 copy.128
  7.4 0.3 fusion.10
  7.7 0.7 fusion.31
  9.7 0.8 select_reduce_fusion
  11.3 5.1 %collective-permute-start.4 = (s32[1,513]{1,0:T(1,128)S(1)}, s32[1,513]{1,0:T(1,128)S(1)}, u32[]{:S(2)}, u32[]{:S(2)}) collective-permute-start(s32[1,513]{1,0:T(1,128)S(1)} %pad_add_fusion.1), channel_id=1, source_target_pairs={{0,12},{4,8},{8,4},{12,0},{1,13},{5,9},{9,5},{13,1},{2,14},{6,10},... | collective-permute-start | bytes 6164 | tf_op jit(solution)/shard_map/ppermute | solution.py:190
  16.5 0.6 collective-permute-start.2
  17.1 0.7 copy.127
  18.0 2.0 collective-permute-done.2
  20.1 0.8 collective-permute-done.3
  20.9 5.1 %gather.7 = bf16[288,2048]{1,0:T(8,128)(2,1)} custom-call(s32[1,1024]{1,0:T(1,128)S(1)} %compare_select_fusion.7.refs_0_, bf16[1024,2048]{1,0:T(8,128)(2,1)} %bitcast.58), custom_call_target="tpu_custom_call" | custom-call | flops 1024 | bytes 1024 | tf_op jit(solution)/shard_map/gather/pallas_call | solution.py:23
  26.0 2.1 collective-permute-start.5
  28.1 3.8 %gather.8 = bf16[448,2048]{1,0:T(8,128)(2,1)} custom-call(s32[1,1024]{1,0:T(1,128)S(1)} %compare_select_fusion.7.refs_0_, bf16[1024,2048]{1,0:T(8,128)(2,1)S(1)} %bitcast.60), custom_call_target="tpu_custom_call" | custom-call | flops 1024 | bytes 1024 | tf_op jit(solution)/shard_map/gather/pallas_call | solution.py:23
  31.9 5.4 %gather.9 = (bf16[224,2048]{1,0:T(8,128)(2,1)S(1)}, bf16[512,2048]{1,0:T(8,128)(2,1)S(1)}, bf16[224,2048]{1,0:T(8,128)(2,1)S(1)}) custom-call(s32[1,1024]{1,0:T(1,128)S(1)} %compare_select_fusion.7.refs_0_, bf16[1024,2048]{1,0:T(8,128)(2,1)S(1)} %bitcast.61), custom_call_target="tpu_custom_call" | custom-call | flops 1024 | bytes 1024 | tf_op jit(solution)/shard_map/gather/pallas_call | solution.py:23
  37.3 0.9 copy-done.3
  38.3 0.9 copy-done.4
  39.2 12.3 %base.1 = bf16[4,1024,512]{2,1,0:T(8,128)(2,1)S(1)} custom-call(s32[4]{0:T(128)S(1)} %iota.37.order_ref, bf16[1024,2048]{1,0:T(8,128)(2,1)S(1)} %bitcast.62, bf16[2048,2048]{1,0:T(8,128)(2,1)} %weight_ref.1), custom_call_target="tpu_custom_call" | custom-call | flops 1024 | bytes 1024 | tf_op jit(solution)/shard_map/base/pallas_call | solution.py:141
  51.5 2.0 copy-done.1
  53.5 0.1 copy.105
  53.7 0.1 copy.99
  53.8 4.9 %all-to-all-start.1 = ((bf16[4,1024,512]{2,1,0:T(8,128)(2,1)}), bf16[4,1024,512]{2,1,0:T(8,128)(2,1)}, u32[]{:S(2)}, u32[]{:S(2)}) async-start(bf16[4,1024,512]{2,1,0:T(8,128)(2,1)} %copy-done.1), calls=%async_computation.1 | async-start | bytes 8388608 | tf_op jit(solution)/shard_map/all_to_all | solution.py:286
  58.9 0.6 slice.63
  59.4 0.5 slice.64
  59.9 0.6 slice.65
  62.4 2.9 %collective-permute-start.6 = (s32[]{:T(128)}, s32[]{:T(128)}, u32[]{:S(2)}, u32[]{:S(2)}) collective-permute-start(s32[]{:T(128)} %reduce_max.24), channel_id=1, source_target_pairs={{0,16},{16,0},{1,17},{17,1},{2,18},{18,2},{3,19},{19,3},{4,20},{20... | collective-permute-start | bytes 20 | tf_op jit(solution)/shard_map/ppermute | solution.py:293
  65.5 0.1 copy.110
  65.8 0.2 collective-permute-done.6
  66.6 11.5 %collective-permute-done.5.refs_2_ = bf16[288,2048]{1,0:T(8,128)(2,1)} collective-permute-done((bf16[288,2048]{1,0:T(8,128)(2,1)}, bf16[288,2048]{1,0:T(8,128)(2,1)}, u32[]{:S(2)}, u32[]{:S(2)}) %collective-permute-start.5) | collective-permute-done | bytes 1179680 | tf_op jit(solution)/shard_map/ppermute | solution.py:190
  78.1 2.6 %collective-permute-start.7 = (bf16[224,2048]{1,0:T(8,128)(2,1)}, bf16[224,2048]{1,0:T(8,128)(2,1)}, u32[]{:S(2)}, u32[]{:S(2)}) collective-permute-start(bf16[224,2048]{1,0:T(8,128)(2,1)} %copy-done.4), channel_id=1, source_target_pairs={{0,12},{4,8},{8,4},{12,0},{1,13},{5,9},{9,5},{13,1},{2,14},{6,10},... | collective-permute-start | bytes 2752520 | tf_op jit(solution)/shard_map/ppermute | solution.py:190
  80.7 8.0 %down.9 = bf16[288,256]{1,0:T(8,128)(2,1)S(1)} custom-call(s32[8]{0:T(128)S(1)} %copy-done.11, s32[288,1]{1,0:T(8,128)S(1)} %slice.79.refs_1_.refs_0_, bf16[288,2048]{1,0:T(8,128)(2,1)} %collective-permute-done.5.refs_2_, bf16[8,2048,256]{2,1,0:T(8,128)(2,1)} %refs_4_.1), custom_call_target="tpu_custom_call" | custom-call | flops 1024 | bytes 1024 | tf_op jit(solution)/shard_map/down/pallas_call | solution.py:66
  88.8 22.1 %all-gather.1 = bf16[1152,256]{1,0:T(8,128)(2,1)S(1)} all-gather(bf16[288,256]{1,0:T(8,128)(2,1)S(1)} %down.9), channel_id=3, replica_groups=mesh['groups'=2,'inst'=4,'tp'=4] {'tp'}, dimensions={0}, use_global_device_ids=true | all-gather | bytes 737280 | tf_op jit(solution)/shard_map/all_gather | solution.py:266
  110.9 0.6 up.10
  111.4 9.6 %down.10 = bf16[512,256]{1,0:T(8,128)(2,1)} custom-call(s32[8]{0:T(128)S(1)} %copy-done.11, s32[512,1]{1,0:T(8,128)S(1)} %and_select_fusion.2.refs_1_.refs_0_, bf16[512,2048]{1,0:T(8,128)(2,1)S(1)} %get-tuple-element.204.refs_2_, bf16[8,2048,256]{2,1,0:T(8,128)(2,1)} %refs_4_.1), custom_call_target="tpu_custom_call" | custom-call | flops 1024 | bytes 1024 | tf_op jit(solution)/shard_map/down/pallas_call | solution.py:66
  121.0 0.8 collective-permute-start.9
  121.8 7.6 %down.11 = bf16[224,256]{1,0:T(8,128)(2,1)S(1)} custom-call(s32[8]{0:T(128)S(1)} %copy-done.11, s32[224,1]{1,0:T(8,128)S(1)} %slice.83.refs_1_.refs_0_, bf16[224,2048]{1,0:T(8,128)(2,1)} %collective-permute-done.7.refs_2_, bf16[8,2048,256]{2,1,0:T(8,128)(2,1)} %refs_4_.1), custom_call_target="tpu_custom_call" | custom-call | flops 1024 | bytes 1024 | tf_op jit(solution)/shard_map/down/pallas_call | solution.py:66
  129.4 6.7 %all-gather.2 = bf16[896,256]{1,0:T(8,128)(2,1)S(1)} all-gather(bf16[224,256]{1,0:T(8,128)(2,1)S(1)} %down.11), channel_id=4, replica_groups=mesh['groups'=2,'inst'=4,'tp'=4] {'tp'}, dimensions={0}, use_global_device_ids=true | all-gather | bytes 573440 | tf_op jit(solution)/shard_map/all_gather | solution.py:266
  136.1 1.2 up.11
  137.2 9.1 %down.12 = bf16[448,256]{1,0:T(8,128)(2,1)S(1)} custom-call(s32[8]{0:T(128)S(1)} %copy-done.11, s32[448,1]{1,0:T(8,128)S(1)} %and_select_fusion.4.refs_1_.refs_0_, bf16[448,2048]{1,0:T(8,128)(2,1)} %collective-permute-done.10.refs_2_, bf16[8,2048,256]{2,1,0:T(8,128)(2,1)} %refs_4_.1), custom_call_target="tpu_custom_call" | custom-call | flops 1024 | bytes 1024 | tf_op jit(solution)/shard_map/down/pallas_call | solution.py:66
  146.4 9.4 %all-gather.3 = bf16[1792,256]{1,0:T(8,128)(2,1)S(1)} all-gather(bf16[448,256]{1,0:T(8,128)(2,1)S(1)} %down.12), channel_id=5, replica_groups=mesh['groups'=2,'inst'=4,'tp'=4] {'tp'}, dimensions={0}, use_global_device_ids=true | all-gather | bytes 1146880 | tf_op jit(solution)/shard_map/all_gather | solution.py:266
  155.8 0.7 up.12
  156.6 2.1 collective-permute-start.12
  158.8 1.6 collective-permute-start.11
  160.5 4.6 %collective-permute-done.9.refs_3_ = bf16[224,2048]{1,0:T(8,128)(2,1)S(1)} collective-permute-done((bf16[224,2048]{1,0:T(8,128)(2,1)}, bf16[224,2048]{1,0:T(8,128)(2,1)S(1)}, u32[]{:S(2)}, u32[]{:S(2)}) %collective-permute-start.9) | collective-permute-done | bytes 917536 | tf_op jit(solution)/shard_map/ppermute | solution.py:190
  165.0 9.2 %down.13 = bf16[512,256]{1,0:T(8,128)(2,1)S(1)} custom-call(s32[8]{0:T(128)S(1)} %copy-done.11, s32[512,1]{1,0:T(8,128)S(1)} %copy.113.refs_1_, bf16[288,2048]{1,0:T(8,128)(2,1)} %collective-permute-done.8.refs_2_, bf16[224,2048]{1,0:T(8,128)(2,1)S(1)} %collective-permute-done.9.refs_3_, bf16[8,2048,256]{2,1,0:T(8,128)(2,1)} %refs_4_.1), custom_call_target="tpu_custom_call" | custom-call | flops 1024 | bytes 1024 | tf_op jit(solution)/shard_map/down/pallas_call | solution.py:66
  174.3 6.7 %all-gather.4 = bf16[1152,256]{1,0:T(8,128)(2,1)S(1)} all-gather(bf16[288,256]{1,0:T(8,128)(2,1)S(1)} %slice.85), channel_id=6, replica_groups=mesh['groups'=2,'inst'=4,'tp'=4] {'tp'}, dimensions={0}, use_global_device_ids=true | all-gather | bytes 737280 | tf_op jit(solution)/shard_map/all_gather | solution.py:266
  181.0 0.6 up.13
  181.7 7.1 %all-gather.5 = bf16[896,256]{1,0:T(8,128)(2,1)S(1)} all-gather(bf16[224,256]{1,0:T(8,128)(2,1)S(1)} %slice.84), channel_id=7, replica_groups=mesh['groups'=2,'inst'=4,'tp'=4] {'tp'}, dimensions={0}, use_global_device_ids=true | all-gather | bytes 573440 | tf_op jit(solution)/shard_map/all_gather | solution.py:266
  188.8 1.7 up.14
  190.5 0.4 collective-permute-done.13
  191.0 0.2 copy.125
  191.2 0.2 copy.114
  191.5 0.7 select_select_fusion.refs_1_
  192.2 0.2 copy.126
  192.4 2.3 collective-permute-start.14
  194.6 0.7 collective-permute-start.15
  195.3 4.5 %convert_reduce_fusion = f32[1024,512]{1,0:T(8,128)} fusion(bf16[4,1024,512]{2,1,0:T(8,128)(2,1)} %all-to-all-done.1), kind=kLoop, calls=%fused_computation.13 | loop fusion | flops 3670016 | bytes 6291456 | tf_op jit(solution)/shard_map/reduce_sum | solution.py:386
  199.8 7.8 %all-gather.10.cloned.1.call-done = bf16[2048,256]{1,0:T(8,128)(2,1)} async-done(((bf16[512,256]{1,0:T(8,128)(2,1)}), bf16[2048,256]{1,0:T(8,128)(2,1)}) %all-gather.10.cloned.1.call-update) | async-done | bytes 1048592 | tf_op jit(solution)/shard_map/all_gather | solution.py:266
  207.7 1.2 copy-done.2
  208.9 0.8 up.15
  209.7 0.8 copy-done.10
  210.5 3.7 %fusion.7 = f32[1024,512]{1,0:T(8,128)} fusion(f32[1024,512]{1,0:T(8,128)S(1)} %copy-done.10, s32[1024]{0:T(1024)S(1)} %select_select_fusion.1, bf16[448,512]{1,0:T(8,128)(2,1)} %collective-permute-done.12, bf16[512,512]{1,0:T(8,128)(2,1)S(1)} %up.15), kind=kOutput, calls=%fused_computation.22 | convolution fusion | flops 1010106368 | bytes 5181440 | tf_op jit(solution)/shard_map/dot_general | solution.py:254
  214.2 2.1 convolution_add_fusion.1.refs_0_
  216.3 2.1 collective-permute-done.15.refs_3_
  218.4 1.7 finish.1
  220.1 1.1 reshape.627
  (65 shorter events, 1.4 us)
Async XLA Ops:
  11.3 8.8 %collective-permute-start.4 = (s32[1,513]{1,0:T(1,128)S(1)}, s32[1,513]{1,0:T(1,128)S(1)}, u32[]{:S(2)}, u32[]{:S(2)}) collective-permute-start(s32[1,513]{1,0:T(1,128)S(1)} %pad_add_fusion.1), channel_id=1, source_target_pairs={{0,12},{4,8},{8,4},{12,0},{1,13},{5,9},{9,5},{13,1},{2,14},{6,10},... | collective-permute-start | bytes 6164 | tf_op jit(solution)/shard_map/ppermute | solution.py:190
  16.4 4.5 %collective-permute-start.3 = (s32[1,513]{1,0:T(1,128)S(1)}, s32[1,513]{1,0:T(1,128)S(1)}, u32[]{:S(2)}, u32[]{:S(2)}) collective-permute-start(s32[1,513]{1,0:T(1,128)S(1)} %pad_add_fusion), channel_id=1, source_target_pairs={{0,8},{4,12},{8,0},{12,4},{1,9},{5,13},{9,1},{13,5},{2,10},{6,14},... | collective-permute-start | bytes 6164 | tf_op jit(solution)/shard_map/ppermute | solution.py:190
  16.5 3.6 %collective-permute-start.2 = (s32[1,449]{1,0:T(1,128)S(1)}, s32[1,449]{1,0:T(1,128)S(1)}, u32[]{:S(2)}, u32[]{:S(2)}) collective-permute-start(s32[1,449]{1,0:T(1,128)S(1)} %pad_add_fusion.2), channel_id=1, source_target_pairs={{0,4},{4,0},{8,12},{12,8},{1,5},{5,1},{9,13},{13,9},{2,6},{6,2},{1... | collective-permute-start | bytes 5396 | tf_op jit(solution)/shard_map/ppermute | solution.py:190
  20.9 7.2 %copy-start.5 = (bf16[4,256,2048]{2,1,0:T(8,128)(2,1)S(1)}, bf16[4,256,2048]{2,1,0:T(8,128)(2,1)}, u32[]{:S(2)}) copy-start(bf16[4,256,2048]{2,1,0:T(8,128)(2,1)} %param.8) | copy-start | bytes 12582916
  26.0 52.2 %collective-permute-start.5 = (bf16[288,2048]{1,0:T(8,128)(2,1)}, bf16[288,2048]{1,0:T(8,128)(2,1)}, u32[]{:S(2)}, u32[]{:S(2)}) collective-permute-start(bf16[288,2048]{1,0:T(8,128)(2,1)} %gather.7), channel_id=1, source_target_pairs={{0,8},{4,12},{8,0},{12,4},{1,9},{5,13},{9,1},{13,5},{2,10},{6,14},... | collective-permute-start | bytes 3538952 | tf_op jit(solution)/shard_map/ppermute | solution.py:190
  31.9 105.3 %collective-permute-start.10 = (bf16[448,2048]{1,0:T(8,128)(2,1)}, bf16[448,2048]{1,0:T(8,128)(2,1)}, u32[]{:S(2)}, u32[]{:S(2)}) collective-permute-start(bf16[448,2048]{1,0:T(8,128)(2,1)} %gather.8), channel_id=1, source_target_pairs={{0,4},{4,0},{8,12},{12,8},{1,5},{5,1},{9,13},{13,9},{2,6},{6,2},{1... | collective-permute-start | bytes 5505032 | tf_op jit(solution)/shard_map/ppermute | solution.py:190
  37.3 1.0 copy-start.3
  38.3 0.9 copy-start.4
  51.5 2.0 copy-start.1
  53.8 127.9 %all-to-all-start.1 = ((bf16[4,1024,512]{2,1,0:T(8,128)(2,1)}), bf16[4,1024,512]{2,1,0:T(8,128)(2,1)}, u32[]{:S(2)}, u32[]{:S(2)}) async-start(bf16[4,1024,512]{2,1,0:T(8,128)(2,1)} %copy-done.1), calls=%async_computation.1 | async-start | bytes 8388608 | tf_op jit(solution)/shard_map/all_to_all | solution.py:286
  58.7 22.0 %copy-start.11 = (s32[8]{0:T(128)S(1)}, s32[8]{0:T(128)}, u32[]{:S(2)}) copy-start(s32[8]{0:T(128)} %refs_0_.9) | copy-start | bytes 100
  58.7 149.0 %all-gather.10.cloned.1.call-start = ((), (), s32[]{:S(2)}) async-start(), calls=%async_computation.2 | async-start | bytes 1310720 | tf_op jit(solution)/shard_map/all_gather | solution.py:266
  62.4 3.6 %collective-permute-start.6 = (s32[]{:T(128)}, s32[]{:T(128)}, u32[]{:S(2)}, u32[]{:S(2)}) collective-permute-start(s32[]{:T(128)} %reduce_max.24), channel_id=1, source_target_pairs={{0,16},{16,0},{1,17},{17,1},{2,18},{18,2},{3,19},{19,3},{4,20},{20... | collective-permute-start | bytes 20 | tf_op jit(solution)/shard_map/ppermute | solution.py:293
  78.1 32.7 %copy-start.6 = (bf16[8,2,128,256]{3,2,1,0:T(8,128)(2,1)S(1)}, bf16[8,2,128,256]{3,2,1,0:T(8,128)(2,1)}, u32[]{:S(2)}) copy-start(bf16[8,2,128,256]{3,2,1,0:T(8,128)(2,1)} %refs_2_.11) | copy-start | bytes 3145732
  78.1 42.9 %collective-permute-start.7 = (bf16[224,2048]{1,0:T(8,128)(2,1)}, bf16[224,2048]{1,0:T(8,128)(2,1)}, u32[]{:S(2)}, u32[]{:S(2)}) collective-permute-start(bf16[224,2048]{1,0:T(8,128)(2,1)} %copy-done.4), channel_id=1, source_target_pairs={{0,12},{4,8},{8,4},{12,0},{1,13},{5,9},{9,5},{13,1},{2,14},{6,10},... | collective-permute-start | bytes 2752520 | tf_op jit(solution)/shard_map/ppermute | solution.py:190
  80.7 79.7 %collective-permute-start.8 = (bf16[288,2048]{1,0:T(8,128)(2,1)}, bf16[288,2048]{1,0:T(8,128)(2,1)}, u32[]{:S(2)}, u32[]{:S(2)}) collective-permute-start(bf16[288,2048]{1,0:T(8,128)(2,1)} %collective-permute-done.5.refs_2_), channel_id=1, source_target_pairs={{0,4},{4,0},{8,12},{12,8},{1,5},{5,1},{9,13},{13,9},{2,6},{6,2},{1... | collective-permute-start | bytes 3538952 | tf_op jit(solution)/shard_map/ppermute | solution.py:190
  121.0 15.1 %copy-start.7 = (bf16[8,2,128,256]{3,2,1,0:T(8,128)(2,1)S(1)}, bf16[8,2,128,256]{3,2,1,0:T(8,128)(2,1)}, u32[]{:S(2)}) copy-start(bf16[8,2,128,256]{3,2,1,0:T(8,128)(2,1)} %refs_2_.11) | copy-start | bytes 3145732
  121.0 44.0 %collective-permute-start.9 = (bf16[224,2048]{1,0:T(8,128)(2,1)}, bf16[224,2048]{1,0:T(8,128)(2,1)S(1)}, u32[]{:S(2)}, u32[]{:S(2)}) collective-permute-start(bf16[224,2048]{1,0:T(8,128)(2,1)} %copy-done.3), channel_id=1, source_target_pairs={{0,8},{4,12},{8,0},{12,4},{1,9},{5,13},{9,1},{13,5},{2,10},{6,14},... | collective-permute-start | bytes 2752520 | tf_op jit(solution)/shard_map/ppermute | solution.py:190
  156.6 25.1 %collective-permute-start.12 = (bf16[448,512]{1,0:T(8,128)(2,1)S(1)}, bf16[448,512]{1,0:T(8,128)(2,1)}, u32[]{:S(2)}, u32[]{:S(2)}) collective-permute-start(bf16[448,512]{1,0:T(8,128)(2,1)S(1)} %up.12), channel_id=1, source_target_pairs={{0,4},{4,0},{8,12},{12,8},{1,5},{5,1},{9,13},{13,9},{2,6},{6,2},{1... | collective-permute-start | bytes 1376264 | tf_op jit(solution)/shard_map/ppermute | solution.py:190
  158.8 22.2 %copy-start.8 = (bf16[8,2,128,256]{3,2,1,0:T(8,128)(2,1)S(1)}, bf16[8,2,128,256]{3,2,1,0:T(8,128)(2,1)}, u32[]{:S(2)}) copy-start(bf16[8,2,128,256]{3,2,1,0:T(8,128)(2,1)} %refs_2_.11) | copy-start | bytes 3145732
  158.8 22.9 %collective-permute-start.11 = (bf16[224,512]{1,0:T(8,128)(2,1)}, bf16[224,512]{1,0:T(8,128)(2,1)S(1)}, u32[]{:S(2)}, u32[]{:S(2)}) collective-permute-start(bf16[224,512]{1,0:T(8,128)(2,1)} %up.11), channel_id=1, source_target_pairs={{0,12},{4,8},{8,4},{12,0},{1,13},{5,9},{9,5},{13,1},{2,14},{6,10},... | collective-permute-start | bytes 688136 | tf_op jit(solution)/shard_map/ppermute | solution.py:190
  181.6 9.3 %collective-permute-start.13 = (bf16[288,512]{1,0:T(8,128)(2,1)S(1)}, bf16[288,512]{1,0:T(8,128)(2,1)S(1)}, u32[]{:S(2)}, u32[]{:S(2)}) collective-permute-start(bf16[288,512]{1,0:T(8,128)(2,1)S(1)} %up.13), channel_id=1, source_target_pairs={{0,4},{4,0},{8,12},{12,8},{1,5},{5,1},{9,13},{13,9},{2,6},{6,2},{1... | collective-permute-start | bytes 884744 | tf_op jit(solution)/shard_map/ppermute | solution.py:190
  192.4 15.3 %copy-start.9 = (bf16[8,2,128,256]{3,2,1,0:T(8,128)(2,1)S(1)}, bf16[8,2,128,256]{3,2,1,0:T(8,128)(2,1)}, u32[]{:S(2)}) copy-start(bf16[8,2,128,256]{3,2,1,0:T(8,128)(2,1)} %refs_2_.11) | copy-start | bytes 3145732
  192.4 23.9 %collective-permute-start.14 = (bf16[224,512]{1,0:T(8,128)(2,1)S(1)}, bf16[224,512]{1,0:T(8,128)(2,1)S(1)}, u32[]{:S(2)}, u32[]{:S(2)}) collective-permute-start(bf16[224,512]{1,0:T(8,128)(2,1)S(1)} %up.14), channel_id=1, source_target_pairs={{0,8},{4,12},{8,0},{12,4},{1,9},{5,13},{9,1},{13,5},{2,10},{6,14},... | collective-permute-start | bytes 688136 | tf_op jit(solution)/shard_map/ppermute | solution.py:190
  194.6 23.7 %collective-permute-start.15 = (bf16[288,512]{1,0:T(8,128)(2,1)S(1)}, bf16[288,512]{1,0:T(8,128)(2,1)S(1)}, u32[]{:S(2)}, u32[]{:S(2)}) collective-permute-start(bf16[288,512]{1,0:T(8,128)(2,1)S(1)} %add.396), channel_id=1, source_target_pairs={{0,8},{4,12},{8,0},{12,4},{1,9},{5,13},{9,1},{13,5},{2,10},{6,14},... | collective-permute-start | bytes 884744 | tf_op jit(solution)/shard_map/ppermute | solution.py:190
  207.7 1.2 copy-start.2
  208.9 1.6 copy-start.10
  210.5 3.7 %copy-start.12 = (u32[32]{0:T(128)S(1)}, u32[32]{0:T(128)}, u32[]{:S(2)}) copy-start(u32[32]{0:T(128)} %constant.208) | copy-start | bytes 388
Sparse Core Ops, SparseCore 0:
  191.1 16.5 all-gather.9
where the time goes:
time: 229 us; the launch traced here: 228 us
  Pallas kernels  77.5 us (34%)
  blocking collectives  52 us (23%)
  waiting for transfers between devices  29.5 us (13%)
  starting transfers between devices  25.8 us (11%)
  between operations  18.3 us (8%)
  local copies, waits for them, and re-layouts  12.3 us (5%)
  other arithmetic  6.65 us (3%)
  matrix products  6.06 us (3%)
    all_gather x5, blocking collectives, gathered(): return lax.all_gather(part, 'tp', axis=0, tiled=False)  52 us
    pallas_call x5, Pallas kernels, down(): pl.pallas_call(lambda *refs: down_kernel(len(xs), *refs), out_shape=jax.S...  43.6 us
    ppermute x13, waiting for transfers between devices, swap(): return lax.ppermute(x, axis, [(i, i ^ distance) for i in range(count)])  21.4 us
    ppermute x13, starting transfers between devices, swap(): return lax.ppermute(x, axis, [(i, i ^ distance) for i in range(count)])  18 us
    pallas_call x3, Pallas kernels, gather(): pl.pallas_call(lambda *refs: gather_kernel(starts, *refs), out_shape=[jax...  14.3 us
    pallas_call x1, Pallas kernels, base_blocks(): pl.pallas_call(base_kernel, out_shape=[jax.ShapeDtypeStruct((share, rows,...  12.3 us
    all_gather x1, waiting for transfers between devices, gathered(): return lax.all_gather(part, 'tp', axis=0, tiled=False)  7.84 us
    unnamed x26, local copies, waits for them, and re-layouts  7.25 us
  transfers between devices with their start and end apart: 16, of which 8 were waited for; matrix products, arithmetic and copies ran while one was open for 7% of the time, Pallas kernels for 31%

commit v1 on v0

--- a/solution.py
+++ b/solution.py
@@ -49,10 +49,14 @@
         total_ref[...] = jnp.zeros_like(total_ref)
 
     for x_ref, (low, high) in zip(xs, spans([x.shape[0] for x in xs])):
-        part = jnp.dot(x_ref[...], weight_ref[0], preferred_element_type=jnp.float32)
-        column = lax.broadcasted_iota(jnp.int32, part.shape, 1) % (part.shape[1] // 2)
-        keep = (id_ref[low:high] == adapter) & (column < ranks_ref[adapter])
-        total_ref[low:high] += jnp.where(keep, part, 0.0)
+        kept = total_ref[low:high]
+        for n in range(weight_ref.shape[0]):
+            mine = adapter * weight_ref.shape[0] + n
+            part = jnp.dot(x_ref[...], weight_ref[n], preferred_element_type=jnp.float32)
+            column = lax.broadcasted_iota(jnp.int32, part.shape, 1) % (part.shape[1] // 2)
+            keep = (id_ref[low:high] == mine) & (column < ranks_ref[mine])
+            kept = jnp.where(keep, part, kept)
+        total_ref[low:high] = kept
 
     @pl.when(adapter == pl.num_programs(0) - 1)
     def _():
@@ -66,10 +70,10 @@
     return pl.pallas_call(
         lambda *refs: down_kernel(len(xs), *refs),
         out_shape=jax.ShapeDtypeStruct((rows, rank2), jnp.bfloat16),
-        grid=(adapters,),
+        grid=(adapters // 2,),
         in_specs=[pl.BlockSpec(memory_space=pltpu.SMEM), pl.BlockSpec((rows, 1), fixed)]
         + [pl.BlockSpec(x.shape, fixed) for x in xs]
-        + [pl.BlockSpec((1, width, rank2), lambda a: (a, 0, 0))],
+        + [pl.BlockSpec((2, width, rank2), lambda a: (a, 0, 0))],
         out_specs=pl.BlockSpec((rows, rank2), fixed),
         scratch_shapes=[pltpu.VMEM((rows, rank2), jnp.float32)],
         compiler_params=pltpu.CompilerParams(vmem_limit_bytes=VMEM),
@@ -331,62 +335,66 @@
     (g_flex,) = gather([base_flex], [flex_cap], target, x)
     r_flex = swap(g_flex, "inst", 2)
     x, target, _ = together(x, target, g_flex)
-    (g_near,) = gather([base_near], [near_cap], target, x)
-    r_near = swap(g_near, "inst", 1)
+    near = near_cap // 2
+    (g_na,) = gather([base_near], [near], target, x)
+    r_na = swap(g_na, "inst", 1)
     most = jnp.max(jnp.concatenate([over] + [g[:, -1:] for g in (got1, got2, got3)], axis=1))
     trips = (largest(most, "groups") + chunk - 1) // chunk
     k_1, k_2, k_3 = held_ids(got1[:, :-1]), held_ids(got2[:, :-1]), held_ids(got3[:, :-1])
     k_2, k_flex = k_2[:far_cap], k_2[far_cap:]
     k_on, k_3 = k_3[:flex_cap], k_3[flex_cap:]
     k_own = held_ids(all_ids[:, :own_cap])
-    k_on_2 = jnp.concatenate([k_on, k_2], axis=0)
-
-    x, target, _ = together(x, target, g_near)
-    g_3, g_own, g_2 = gather(
-        [base_far3, 0, base_far2], [far_cap, own_cap, far_cap], target, x
+    k_na, k_nb = k_1[:near_cap // 2], k_1[near_cap // 2 :]
+    k_3_na = jnp.concatenate([k_3, k_na], axis=0)
+    k_2_nb = jnp.concatenate([k_2, k_nb], axis=0)
+
+    x, target, _ = together(x, target, g_na)
+    g_3, g_own, g_2, g_nb = gather(
+        [base_far3, 0, base_far2, base_near + near], [far_cap, own_cap, far_cap, near], target, x
     )
     x, g_own = together(x, g_own)
     part = base_parts(x)
     sent = base_sent(part)
 
-    r_flex, g_3, g_2, trips, k_flex, k_own, k_on_2, k_on, k_3, k_1, k_2, _ = together(
-        r_flex, g_3, g_2, trips, k_flex, k_own, k_on_2, k_on, k_3, k_1, k_2, part
+    r_flex, r_na, g_3, g_2, g_nb, trips, k_flex, k_own, k_on, k_3_na, k_2_nb, _ = together(
+        r_flex, r_na, g_3, g_2, g_nb, trips, k_flex, k_own, k_on, k_3_na, k_2_nb, part
     )
     r_3 = swap(g_3, "inst", 3)
     r_on = swap(r_flex, "inst", 1)
     s_flex = shrink([r_flex], k_flex)
     g_own, s_flex = together(g_own, s_flex)
     s_own = shrink([g_own], k_own)
+    s_flex, s_own = together(s_flex, s_own)
     (d_flex,) = expand([gathered(s_flex)], k_flex, [flex_cap])
 
-    r_3, g_2, s_own, d_flex = together(r_3, g_2, s_own, d_flex)
+    r_3, r_na, g_2, g_nb, s_own, d_flex = together(r_3, r_na, g_2, g_nb, s_own, d_flex)
     r_2 = swap(g_2, "inst", 2)
-    s_3 = shrink([r_3], k_3)
-    (d_3,) = expand([gathered(s_3)], k_3, [far_cap])
-    b_3 = swap(d_3, "inst", 3)
-
-    r_near, d_3 = together(r_near, d_3)
-    s_near = shrink([r_near], k_1)
-    (d_near,) = expand([gathered(s_near)], k_1, [near_cap])
-    b_near = swap(d_near, "inst", 1)
-
-    r_on, r_2, d_near = together(r_on, r_2, d_near)
-    s_on_2 = shrink([r_on, r_2], k_on_2)
-    s_on, s_2 = s_on_2[:flex_cap], s_on_2[flex_cap:]
-    (d_on,) = expand([gathered(s_on)], k_on, [flex_cap])
+    r_nb = swap(g_nb, "inst", 1)
+    s_3_na = shrink([r_3, r_na], k_3_na)
+    d_3, d_na = expand([gathered(s_3_na)], k_3_na, [far_cap, near])
+
+    r_on, d_3, d_na = together(r_on, d_3, d_na)
+    b_3, b_na = swap(d_3, "inst", 3), swap(d_na, "inst", 1)
+    (d_on,) = expand([gathered(shrink([r_on], k_on))], k_on, [flex_cap])
     b_on = swap(d_on, "inst", 1)
-    s_2, d_on, b_3, b_near, sent = together(s_2, d_on, b_3, b_near, sent)
-    (d_2,) = expand([gathered(s_2)], k_2, [far_cap])
-    b_2 = swap(d_2, "inst", 2)
-    b_on, d_2 = together(b_on, d_2)
+
+    r_2, r_nb, d_on = together(r_2, r_nb, d_on)
+    s_2_nb = shrink([r_2, r_nb], k_2_nb)
+    s_2_nb, b_on = together(s_2_nb, b_on)
     back_flex = d_flex + b_on
     b_flex = swap(back_flex, "inst", 2)
-    s_own, sent, b_3, b_near, _ = together(s_own, sent, b_3, b_near, back_flex)
-    (d_own,) = expand([gathered(s_own)], k_own, [own_cap])
+    s_2_nb, _ = together(s_2_nb, back_flex)
+    d_2, d_nb = expand([gathered(s_2_nb)], k_2_nb, [far_cap, near])
+    d_2, d_nb, b_flex, b_3, b_na, e_own = together(d_2, d_nb, b_flex, b_3, b_na, gathered(s_own))
+    b_2, b_nb = swap(d_2, "inst", 2), swap(d_nb, "inst", 1)
+    e_own, sent, b_3, b_na, _ = together(e_own, sent, b_3, b_na, d_2)
+    (d_own,) = expand([e_own], k_own, [own_cap])
     base = jnp.sum(sent.astype(jnp.float32), axis=0)
-    total = add_overflow(base + put(0, jnp.concatenate([d_own, b_near], axis=0)), trips)
+    total = add_overflow(base + put(0, jnp.concatenate([d_own, b_na], axis=0)), trips)
     total = total + put(base_far3, b_3)
-    total = finish(total, target_column, [base_far2, base_flex], [b_2, b_flex])
+    total = finish(
+        total, target_column, [base_far2, base_flex, base_near + near], [b_2, b_flex, b_nb]
+    )
     return total.reshape(steps, step_rows, halves, columns)
 
 

time: 229 us -> 222 us (0.969)
  waiting for transfers between devices: 29.5 us -> 17.8 us
  Pallas kernels: 77.5 us -> 70.7 us
  starting transfers between devices: 25.8 us -> 30.7 us
  blocking collectives: 52 us -> 56.2 us
  local copies, waits for them, and re-layouts: 12.3 us -> 16.4 us
    pallas_call x5, Pallas kernels: 43.6 us -> 34.3 us  [down(): pl.pallas_call(lambda *refs: down_kernel(len(xs), *refs), out_shape=jax.S...]
    all_gather x1, waiting for transfers between devices: 7.84 us -> 0.01 us  [gathered(): return lax.all_gather(part, 'tp', axis=0, tiled=False)]
    ppermute x13 -> x15, starting transfers between devices: 18 us -> 22.7 us  [swap(): return lax.ppermute(x, axis, [(i, i ^ distance) for i in range(count)])]
    all_gather x5 -> x4, blocking collectives: 52 us -> 56.2 us  [gathered(): return lax.all_gather(part, 'tp', axis=0, tiled=False)]
    ppermute x13 -> x15, waiting for transfers between devices: 21.4 us -> 17.7 us  [swap(): return lax.ppermute(x, axis, [(i, i ^ distance) for i in range(count)])]
    unnamed x26 -> x40, local copies, waits for them, and re-layouts: 7.25 us -> 9.72 us
    pallas_call x6 -> x5, Pallas kernels: 5.57 us -> 6.51 us  [up(): pl.pallas_call(lambda *refs: up_kernel(len(parts), *refs), out_shape=[jax...]
  transfers between devices with their start and end apart: 16 -> 18, of which waited for: 8 -> 6; matrix products, arithmetic and copies ran while one was open for 7% -> 7% of each run, Pallas kernels for 31% -> 29%
where the time goes in v1:
time: 222 us; the launch traced here: 221 us
  Pallas kernels  70.7 us (32%)
  blocking collectives  56.2 us (25%)
  starting transfers between devices  30.7 us (14%)
  between operations  18.4 us (8%)
  waiting for transfers between devices  17.8 us (8%)
  local copies, waits for them, and re-layouts  16.4 us (7%)
  other arithmetic  6.29 us (3%)
  matrix products  4.76 us (2%)
    all_gather x4, blocking collectives, gathered(): return lax.all_gather(part, 'tp', axis=0, tiled=False)  56.2 us
    pallas_call x5, Pallas kernels, down(): pl.pallas_call(lambda *refs: down_kernel(len(xs), *refs), out_shape=jax.S...  34.3 us
    ppermute x15, starting transfers between devices, swap(): return lax.ppermute(x, axis, [(i, i ^ distance) for i in range(count)])  22.7 us
    ppermute x15, waiting for transfers between devices, swap(): return lax.ppermute(x, axis, [(i, i ^ distance) for i in range(count)])  17.7 us
    pallas_call x3, Pallas kernels, gather(): pl.pallas_call(lambda *refs: gather_kernel(starts, *refs), out_shape=[jax...  15.5 us
    pallas_call x1, Pallas kernels, base_blocks(): pl.pallas_call(base_kernel, out_shape=[jax.ShapeDtypeStruct((share, rows,...  12.3 us
    unnamed x40, local copies, waits for them, and re-layouts  9.72 us
    pallas_call x5, Pallas kernels, up(): pl.pallas_call(lambda *refs: up_kernel(len(parts), *refs), out_shape=[jax...  6.51 us
  transfers between devices with their start and end apart: 18, of which 6 were waited for; matrix products, arithmetic and copies ran while one was open for 7% of the time, Pallas kernels for 29%

profile of v1, /device:TPU:0, one launch (start us, length us, event | category | flops | bytes accessed | tf_op | source)
XLA Modules:
  0.0 221.1 jit_solution(15808131257807468617)
XLA Ops:
  6.5 0.7 copy.128
  7.4 0.3 fusion.10
  7.7 0.7 fusion.32
  9.7 0.8 select_reduce_fusion
  11.3 5.1 %collective-permute-start.4 = (s32[1,513]{1,0:T(1,128)S(1)}, s32[1,513]{1,0:T(1,128)S(1)}, u32[]{:S(2)}, u32[]{:S(2)}) collective-permute-start(s32[1,513]{1,0:T(1,128)S(1)} %pad_add_fusion.1), channel_id=1, source_target_pairs={{0,12},{4,8},{8,4},{12,0},{1,13},{5,9},{9,5},{13,1},{2,14},{6,10},... | collective-permute-start | bytes 6164 | tf_op jit(solution)/shard_map/ppermute | solution.py:194
  16.5 0.6 collective-permute-start.2
  17.1 0.7 copy.127
  18.1 2.0 collective-permute-done.2
  20.1 0.8 collective-permute-done.3
  20.9 5.1 %gather.7 = bf16[288,2048]{1,0:T(8,128)(2,1)} custom-call(s32[1,1024]{1,0:T(1,128)S(1)} %compare_select_fusion.7.refs_0_, bf16[1024,2048]{1,0:T(8,128)(2,1)} %bitcast.56), custom_call_target="tpu_custom_call" | custom-call | flops 1024 | bytes 1024 | tf_op jit(solution)/shard_map/gather/pallas_call | solution.py:23
  26.0 2.1 collective-permute-start.5
  28.1 2.9 %gather.8 = bf16[224,2048]{1,0:T(8,128)(2,1)} custom-call(s32[1,1024]{1,0:T(1,128)S(1)} %compare_select_fusion.7.refs_0_, bf16[1024,2048]{1,0:T(8,128)(2,1)S(1)} %bitcast.59), custom_call_target="tpu_custom_call" | custom-call | flops 1024 | bytes 1024 | tf_op jit(solution)/shard_map/gather/pallas_call | solution.py:23
  31.1 0.1 copy.99
  31.3 7.4 %gather.9 = (bf16[224,2048]{1,0:T(8,128)(2,1)S(1)}, bf16[512,2048]{1,0:T(8,128)(2,1)S(1)}, bf16[224,2048]{1,0:T(8,128)(2,1)S(1)}, bf16[224,2048]{1,0:T(8,128)(2,1)S(1)}) custom-call(s32[1,1024]{1,0:T(1,128)S(1)} %compare_select_fusion.7.refs_0_, bf16[1024,2048]{1,0:T(8,128)(2,1)} %bitcast.57), custom_call_target="tpu_custom_call" | custom-call | flops 1024 | bytes 1024 | tf_op jit(solution)/shard_map/gather/pallas_call | solution.py:23
  38.7 0.9 copy-done.3
  39.7 0.9 copy-done.4
  40.6 0.9 copy-done.5
  41.5 12.3 %base.1 = bf16[4,1024,512]{2,1,0:T(8,128)(2,1)S(1)} custom-call(s32[4]{0:T(128)S(1)} %iota.37.order_ref, bf16[1024,2048]{1,0:T(8,128)(2,1)S(1)} %bitcast.60, bf16[2048,2048]{1,0:T(8,128)(2,1)} %weight_ref.1), custom_call_target="tpu_custom_call" | custom-call | flops 1024 | bytes 1024 | tf_op jit(solution)/shard_map/base/pallas_call | solution.py:145
  53.9 2.0 copy-done.1
  55.8 0.5 slice.64
  56.3 0.6 slice.65
  57.1 0.6 slice.63
  59.6 2.9 %collective-permute-start.7 = (s32[]{:T(128)}, s32[]{:T(128)}, u32[]{:S(2)}, u32[]{:S(2)}) collective-permute-start(s32[]{:T(128)} %reduce_max.24), channel_id=1, source_target_pairs={{0,16},{16,0},{1,17},{17,1},{2,18},{18,2},{3,19},{19,3},{4,20},{20... | collective-permute-start | bytes 20 | tf_op jit(solution)/shard_map/ppermute | solution.py:297
  62.6 5.0 %all-to-all-start.1 = ((bf16[4,1024,512]{2,1,0:T(8,128)(2,1)}), bf16[4,1024,512]{2,1,0:T(8,128)(2,1)}, u32[]{:S(2)}, u32[]{:S(2)}) async-start(bf16[4,1024,512]{2,1,0:T(8,128)(2,1)} %copy-done.1), calls=%async_computation.1 | async-start | bytes 8388608 | tf_op jit(solution)/shard_map/all_to_all | solution.py:290
  68.6 3.1 %collective-permute-done.6.refs_3_ = bf16[224,2048]{1,0:T(8,128)(2,1)} collective-permute-done((bf16[224,2048]{1,0:T(8,128)(2,1)}, bf16[224,2048]{1,0:T(8,128)(2,1)}, u32[]{:S(2)}, u32[]{:S(2)}) %collective-permute-start.6) | collective-permute-done | bytes 917536 | tf_op jit(solution)/shard_map/ppermute | solution.py:194
  71.7 6.4 %collective-permute-done.5.refs_2_ = bf16[288,2048]{1,0:T(8,128)(2,1)} collective-permute-done((bf16[288,2048]{1,0:T(8,128)(2,1)}, bf16[288,2048]{1,0:T(8,128)(2,1)}, u32[]{:S(2)}, u32[]{:S(2)}) %collective-permute-start.5) | collective-permute-done | bytes 1179680 | tf_op jit(solution)/shard_map/ppermute | solution.py:194
  78.1 2.6 %collective-permute-start.8 = (bf16[224,2048]{1,0:T(8,128)(2,1)}, bf16[224,2048]{1,0:T(8,128)(2,1)}, u32[]{:S(2)}, u32[]{:S(2)}) collective-permute-start(bf16[224,2048]{1,0:T(8,128)(2,1)} %copy-done.5), channel_id=1, source_target_pairs={{0,12},{4,8},{8,4},{12,0},{1,13},{5,9},{9,5},{13,1},{2,14},{6,10},... | collective-permute-start | bytes 2752520 | tf_op jit(solution)/shard_map/ppermute | solution.py:194
  80.6 6.1 %down.9 = bf16[288,256]{1,0:T(8,128)(2,1)S(1)} custom-call(s32[8]{0:T(128)S(1)} %copy-done.16, s32[288,1]{1,0:T(8,128)S(1)} %slice.79.refs_1_.refs_0_, bf16[288,2048]{1,0:T(8,128)(2,1)} %collective-permute-done.5.refs_2_, bf16[8,2048,256]{2,1,0:T(8,128)(2,1)} %refs_4_.3), custom_call_target="tpu_custom_call" | custom-call | flops 1024 | bytes 1024 | tf_op jit(solution)/shard_map/down/pallas_call | solution.py:70
  86.7 7.9 %down.10 = bf16[512,256]{1,0:T(8,128)(2,1)} custom-call(s32[8]{0:T(128)S(1)} %copy-done.16, s32[512,1]{1,0:T(8,128)S(1)} %and_select_fusion.2.refs_1_.refs_0_, bf16[512,2048]{1,0:T(8,128)(2,1)S(1)} %get-tuple-element.224.refs_2_, bf16[8,2048,256]{2,1,0:T(8,128)(2,1)} %refs_4_.3), custom_call_target="tpu_custom_call" | custom-call | flops 1024 | bytes 1024 | tf_op jit(solution)/shard_map/down/pallas_call | solution.py:70
  94.6 25.2 %all-gather.1 = bf16[1152,256]{1,0:T(8,128)(2,1)S(1)} all-gather(bf16[288,256]{1,0:T(8,128)(2,1)S(1)} %down.9), channel_id=3, replica_groups=mesh['groups'=2,'inst'=4,'tp'=4] {'tp'}, dimensions={0}, use_global_device_ids=true | all-gather | bytes 737280 | tf_op jit(solution)/shard_map/all_gather | solution.py:270
  119.8 1.8 up.9
  121.7 1.0 copy.125
  122.7 1.0 copy.114
  123.9 2.1 collective-permute-start.10
  126.0 0.8 collective-permute-start.9
  126.8 7.4 %down.11 = bf16[448,256]{1,0:T(8,128)(2,1)S(1)} custom-call(s32[8]{0:T(128)S(1)} %copy-done.16, s32[448,1]{1,0:T(8,128)S(1)} %copy.111.refs_1_.refs_0_, bf16[224,2048]{1,0:T(8,128)(2,1)} %collective-permute-done.8.refs_2_, bf16[224,2048]{1,0:T(8,128)(2,1)} %collective-permute-done.6.refs_3_, bf16[8,2048,256]{2,1,0:T(8,128)(2,1)} %refs_4_.3), custom_call_target="tpu_custom_call" | custom-call | flops 1024 | bytes 1024 | tf_op jit(solution)/shard_map/down/pallas_call | solution.py:70
  134.2 8.9 %all-gather.2 = bf16[1792,256]{1,0:T(8,128)(2,1)S(1)} all-gather(bf16[448,256]{1,0:T(8,128)(2,1)S(1)} %down.11), channel_id=4, replica_groups=mesh['groups'=2,'inst'=4,'tp'=4] {'tp'}, dimensions={0}, use_global_device_ids=true | all-gather | bytes 1146880 | tf_op jit(solution)/shard_map/all_gather | solution.py:270
  143.1 0.7 up.10
  143.9 6.2 %down.12 = bf16[288,256]{1,0:T(8,128)(2,1)S(1)} custom-call(s32[8]{0:T(128)S(1)} %copy-done.16, s32[288,1]{1,0:T(8,128)S(1)} %slice.81.refs_1_.refs_0_, bf16[288,2048]{1,0:T(8,128)(2,1)} %collective-permute-done.11.refs_2_, bf16[8,2048,256]{2,1,0:T(8,128)(2,1)} %refs_4_.3), custom_call_target="tpu_custom_call" | custom-call | flops 1024 | bytes 1024 | tf_op jit(solution)/shard_map/down/pallas_call | solution.py:70
  150.1 8.0 %all-gather.3 = bf16[1152,256]{1,0:T(8,128)(2,1)S(1)} all-gather(bf16[288,256]{1,0:T(8,128)(2,1)S(1)} %down.12), channel_id=5, replica_groups=mesh['groups'=2,'inst'=4,'tp'=4] {'tp'}, dimensions={0}, use_global_device_ids=true | all-gather | bytes 737280 | tf_op jit(solution)/shard_map/all_gather | solution.py:270
  158.0 1.3 up.11
  159.3 0.3 collective-permute-start.12
  159.6 0.7 select_select_fusion.refs_1_
  160.3 0.2 copy.126
  160.5 0.1 copy.113.refs_1_.refs_0_
  160.7 4.9 %collective-permute-start.14 = (bf16[224,512]{1,0:T(8,128)(2,1)}, bf16[224,512]{1,0:T(8,128)(2,1)S(1)}, u32[]{:S(2)}, u32[]{:S(2)}) collective-permute-start(bf16[224,512]{1,0:T(8,128)(2,1)} %copy-done.6), channel_id=1, source_target_pairs={{0,12},{4,8},{8,4},{12,0},{1,13},{5,9},{9,5},{13,1},{2,14},{6,10},... | collective-permute-start | bytes 688136 | tf_op jit(solution)/shard_map/ppermute | solution.py:194
  165.6 1.1 collective-permute-start.15
  166.7 3.3 %collective-permute-done.9.refs_2_ = bf16[224,2048]{1,0:T(8,128)(2,1)S(1)} collective-permute-done((bf16[224,2048]{1,0:T(8,128)(2,1)}, bf16[224,2048]{1,0:T(8,128)(2,1)S(1)}, u32[]{:S(2)}, u32[]{:S(2)}) %collective-permute-start.9) | collective-permute-done | bytes 917536 | tf_op jit(solution)/shard_map/ppermute | solution.py:194
  170.0 6.8 %down.13 = bf16[448,256]{1,0:T(8,128)(2,1)S(1)} custom-call(s32[8]{0:T(128)S(1)} %copy-done.16, s32[448,1]{1,0:T(8,128)S(1)} %copy.113.refs_1_.refs_0_, bf16[224,2048]{1,0:T(8,128)(2,1)S(1)} %collective-permute-done.9.refs_2_, bf16[224,2048]{1,0:T(8,128)(2,1)S(1)} %collective-permute-done.10.refs_3_, bf16[8,2048,256]{2,1,0:T(8,128)(2,1)} %refs_4_.3), custom_call_target="tpu_custom_call" | custom-call | flops 1024 | bytes 1024 | tf_op jit(solution)/shard_map/down/pallas_call | solution.py:70
  176.8 1.1 add.396
  178.0 14.1 %all-gather.4 = bf16[1792,256]{1,0:T(8,128)(2,1)S(1)} all-gather(bf16[448,256]{1,0:T(8,128)(2,1)S(1)} %down.13), channel_id=6, replica_groups=mesh['groups'=2,'inst'=4,'tp'=4] {'tp'}, dimensions={0}, use_global_device_ids=true | all-gather | bytes 1146880 | tf_op jit(solution)/shard_map/all_gather | solution.py:270
  192.1 0.7 up.12
  192.9 0.7 copy-done.14
  193.5 0.7 copy-done.17
  194.2 2.9 %collective-permute-start.16 = (bf16[224,512]{1,0:T(8,128)(2,1)S(1)}, bf16[224,512]{1,0:T(8,128)(2,1)S(1)}, u32[]{:S(2)}, u32[]{:S(2)}) collective-permute-start(bf16[224,512]{1,0:T(8,128)(2,1)S(1)} %get-tuple-element.250), channel_id=1, source_target_pairs={{0,8},{4,12},{8,0},{12,4},{1,9},{5,13},{9,1},{13,5},{2,10},{6,14},... | collective-permute-start | bytes 688136 | tf_op jit(solution)/shard_map/ppermute | solution.py:194
  197.1 1.2 copy-done.2
  198.4 2.0 up.13
  200.4 3.0 %convert_reduce_fusion = f32[1024,512]{1,0:T(8,128)S(1)} fusion(bf16[4,1024,512]{2,1,0:T(8,128)(2,1)} %all-to-all-done.1), kind=kLoop, calls=%fused_computation.13 | loop fusion | flops 3670016 | bytes 6291456 | tf_op jit(solution)/shard_map/reduce_sum | solution.py:392
  203.6 2.4 %fusion.6 = f32[1024,512]{1,0:T(8,128)} fusion(f32[1024,512]{1,0:T(8,128)S(1)} %convert_reduce_fusion, s32[1024]{0:T(1024)S(1)} %select_select_fusion.1, bf16[224,512]{1,0:T(8,128)(2,1)S(1)} %copy-done.18, bf16[512,512]{1,0:T(8,128)(2,1)S(1)} %up.13), kind=kOutput, calls=%fused_computation.20 | convolution fusion | flops 774537216 | bytes 4952064 | tf_op jit(solution)/shard_map/dot_general | solution.py:258
  206.0 0.9 copy-done.15
  206.9 2.1 convolution_add_fusion.1.refs_0_
  209.0 2.2 collective-permute-done.17.refs_4_
  211.1 2.0 finish.1
  213.2 1.1 reshape.627
  (80 shorter events, 1.7 us)
Async XLA Ops:
  11.3 8.8 %collective-permute-start.4 = (s32[1,513]{1,0:T(1,128)S(1)}, s32[1,513]{1,0:T(1,128)S(1)}, u32[]{:S(2)}, u32[]{:S(2)}) collective-permute-start(s32[1,513]{1,0:T(1,128)S(1)} %pad_add_fusion.1), channel_id=1, source_target_pairs={{0,12},{4,8},{8,4},{12,0},{1,13},{5,9},{9,5},{13,1},{2,14},{6,10},... | collective-permute-start | bytes 6164 | tf_op jit(solution)/shard_map/ppermute | solution.py:194
  16.4 4.5 %collective-permute-start.3 = (s32[1,513]{1,0:T(1,128)S(1)}, s32[1,513]{1,0:T(1,128)S(1)}, u32[]{:S(2)}, u32[]{:S(2)}) collective-permute-start(s32[1,513]{1,0:T(1,128)S(1)} %pad_add_fusion), channel_id=1, source_target_pairs={{0,8},{4,12},{8,0},{12,4},{1,9},{5,13},{9,1},{13,5},{2,10},{6,14},... | collective-permute-start | bytes 6164 | tf_op jit(solution)/shard_map/ppermute | solution.py:194
  16.5 3.6 %collective-permute-start.2 = (s32[1,449]{1,0:T(1,128)S(1)}, s32[1,449]{1,0:T(1,128)S(1)}, u32[]{:S(2)}, u32[]{:S(2)}) collective-permute-start(s32[1,449]{1,0:T(1,128)S(1)} %pad_add_fusion.2), channel_id=1, source_target_pairs={{0,4},{4,0},{8,12},{12,8},{1,5},{5,1},{9,13},{13,9},{2,6},{6,2},{1... | collective-permute-start | bytes 5396 | tf_op jit(solution)/shard_map/ppermute | solution.py:194
  20.9 7.3 %copy-start.7 = (bf16[4,256,2048]{2,1,0:T(8,128)(2,1)S(1)}, bf16[4,256,2048]{2,1,0:T(8,128)(2,1)}, u32[]{:S(2)}) copy-start(bf16[4,256,2048]{2,1,0:T(8,128)(2,1)} %param.8) | copy-start | bytes 12582916
  26.0 52.1 %collective-permute-start.5 = (bf16[288,2048]{1,0:T(8,128)(2,1)}, bf16[288,2048]{1,0:T(8,128)(2,1)}, u32[]{:S(2)}, u32[]{:S(2)}) collective-permute-start(bf16[288,2048]{1,0:T(8,128)(2,1)} %gather.7), channel_id=1, source_target_pairs={{0,8},{4,12},{8,0},{12,4},{1,9},{5,13},{9,1},{13,5},{2,10},{6,14},... | collective-permute-start | bytes 3538952 | tf_op jit(solution)/shard_map/ppermute | solution.py:194
  31.1 40.6 %collective-permute-start.6 = (bf16[224,2048]{1,0:T(8,128)(2,1)}, bf16[224,2048]{1,0:T(8,128)(2,1)}, u32[]{:S(2)}, u32[]{:S(2)}) collective-permute-start(bf16[224,2048]{1,0:T(8,128)(2,1)} %gather.8), channel_id=1, source_target_pairs={{0,4},{4,0},{8,12},{12,8},{1,5},{5,1},{9,13},{13,9},{2,6},{6,2},{1... | collective-permute-start | bytes 2752520 | tf_op jit(solution)/shard_map/ppermute | solution.py:194
  31.3 10.3 %copy-start.8 = (bf16[4,256,2048]{2,1,0:T(8,128)(2,1)S(1)}, bf16[4,256,2048]{2,1,0:T(8,128)(2,1)}, u32[]{:S(2)}) copy-start(bf16[4,256,2048]{2,1,0:T(8,128)(2,1)} %param.8) | copy-start | bytes 12582916
  38.7 1.0 copy-start.3
  39.7 0.9 copy-start.4
  40.6 0.9 copy-start.5
  53.9 2.0 copy-start.1
  59.6 8.4 %collective-permute-start.7 = (s32[]{:T(128)}, s32[]{:T(128)}, u32[]{:S(2)}, u32[]{:S(2)}) collective-permute-start(s32[]{:T(128)} %reduce_max.24), channel_id=1, source_target_pairs={{0,16},{16,0},{1,17},{17,1},{2,18},{18,2},{3,19},{19,3},{4,20},{20... | collective-permute-start | bytes 20 | tf_op jit(solution)/shard_map/ppermute | solution.py:297
  62.6 18.0 %copy-start.16 = (s32[8]{0:T(128)S(1)}, s32[8]{0:T(128)}, u32[]{:S(2)}) copy-start(s32[8]{0:T(128)} %refs_0_.9) | copy-start | bytes 100
  62.6 134.5 %all-to-all-start.1 = ((bf16[4,1024,512]{2,1,0:T(8,128)(2,1)}), bf16[4,1024,512]{2,1,0:T(8,128)(2,1)}, u32[]{:S(2)}, u32[]{:S(2)}) async-start(bf16[4,1024,512]{2,1,0:T(8,128)(2,1)} %copy-done.1), calls=%async_computation.1 | async-start | bytes 8388608 | tf_op jit(solution)/shard_map/all_to_all | solution.py:290
  67.7 126.6 %all-gather.9.cloned.1.call-start = ((), (), s32[]{:S(2)}) async-start(), calls=%async_computation.2 | async-start | bytes 1310720 | tf_op jit(solution)/shard_map/all_gather | solution.py:270
  78.1 43.6 %collective-permute-start.8 = (bf16[224,2048]{1,0:T(8,128)(2,1)}, bf16[224,2048]{1,0:T(8,128)(2,1)}, u32[]{:S(2)}, u32[]{:S(2)}) collective-permute-start(bf16[224,2048]{1,0:T(8,128)(2,1)} %copy-done.5), channel_id=1, source_target_pairs={{0,12},{4,8},{8,4},{12,0},{1,13},{5,9},{9,5},{13,1},{2,14},{6,10},... | collective-permute-start | bytes 2752520 | tf_op jit(solution)/shard_map/ppermute | solution.py:194
  80.6 63.2 %collective-permute-start.11 = (bf16[288,2048]{1,0:T(8,128)(2,1)}, bf16[288,2048]{1,0:T(8,128)(2,1)}, u32[]{:S(2)}, u32[]{:S(2)}) collective-permute-start(bf16[288,2048]{1,0:T(8,128)(2,1)} %collective-permute-done.5.refs_2_), channel_id=1, source_target_pairs={{0,4},{4,0},{8,12},{12,8},{1,5},{5,1},{9,13},{13,9},{2,6},{6,2},{1... | collective-permute-start | bytes 3538952 | tf_op jit(solution)/shard_map/ppermute | solution.py:194
  123.9 19.3 %copy-start.9 = (bf16[8,2,128,256]{3,2,1,0:T(8,128)(2,1)S(1)}, bf16[8,2,128,256]{3,2,1,0:T(8,128)(2,1)}, u32[]{:S(2)}) copy-start(bf16[8,2,128,256]{3,2,1,0:T(8,128)(2,1)} %refs_2_.9) | copy-start | bytes 3145732
  123.9 42.8 %collective-permute-start.10 = (bf16[224,2048]{1,0:T(8,128)(2,1)}, bf16[224,2048]{1,0:T(8,128)(2,1)S(1)}, u32[]{:S(2)}, u32[]{:S(2)}) collective-permute-start(bf16[224,2048]{1,0:T(8,128)(2,1)} %copy-done.4), channel_id=1, source_target_pairs={{0,4},{4,0},{8,12},{12,8},{1,5},{5,1},{9,13},{13,9},{2,6},{6,2},{1... | collective-permute-start | bytes 2752520 | tf_op jit(solution)/shard_map/ppermute | solution.py:194
  126.0 44.0 %collective-permute-start.9 = (bf16[224,2048]{1,0:T(8,128)(2,1)}, bf16[224,2048]{1,0:T(8,128)(2,1)S(1)}, u32[]{:S(2)}, u32[]{:S(2)}) collective-permute-start(bf16[224,2048]{1,0:T(8,128)(2,1)} %copy-done.3), channel_id=1, source_target_pairs={{0,8},{4,12},{8,0},{12,4},{1,9},{5,13},{9,1},{13,5},{2,10},{6,14},... | collective-permute-start | bytes 2752520 | tf_op jit(solution)/shard_map/ppermute | solution.py:194
  143.8 6.2 %copy-start.6 = (bf16[224,512]{1,0:T(8,128)(2,1)}, bf16[224,512]{1,0:T(8,128)(2,1)S(1)}, u32[]{:S(2)}) copy-start(bf16[224,512]{1,0:T(8,128)(2,1)S(1)} %get-tuple-element.244) | copy-start | bytes 688132
  150.0 9.6 %copy-start.12 = (s32[1024,1]{1,0:T(8,128)S(1)}, s32[1024,1]{1,0:T(8,128)}, u32[]{:S(2)}) copy-start(s32[1024,1]{1,0:T(8,128)} %copy.125) | copy-start | bytes 12292
  150.1 9.6 %copy-start.13 = (s32[1024,1]{1,0:T(8,128)S(1)}, s32[1024,1]{1,0:T(8,128)}, u32[]{:S(2)}) copy-start(s32[1024,1]{1,0:T(8,128)} %copy.114) | copy-start | bytes 12292
  159.3 17.5 %collective-permute-start.12 = (bf16[288,512]{1,0:T(8,128)(2,1)}, bf16[288,512]{1,0:T(8,128)(2,1)}, u32[]{:S(2)}, u32[]{:S(2)}) collective-permute-start(bf16[288,512]{1,0:T(8,128)(2,1)} %up.11), channel_id=1, source_target_pairs={{0,4},{4,0},{8,12},{12,8},{1,5},{5,1},{9,13},{13,9},{2,6},{6,2},{1... | collective-permute-start | bytes 884744 | tf_op jit(solution)/shard_map/ppermute | solution.py:194
  160.7 32.2 %collective-permute-start.14 = (bf16[224,512]{1,0:T(8,128)(2,1)}, bf16[224,512]{1,0:T(8,128)(2,1)S(1)}, u32[]{:S(2)}, u32[]{:S(2)}) collective-permute-start(bf16[224,512]{1,0:T(8,128)(2,1)} %copy-done.6), channel_id=1, source_target_pairs={{0,12},{4,8},{8,4},{12,0},{1,13},{5,9},{9,5},{13,1},{2,14},{6,10},... | collective-permute-start | bytes 688136 | tf_op jit(solution)/shard_map/ppermute | solution.py:194
  165.6 27.3 %collective-permute-start.15 = (bf16[224,512]{1,0:T(8,128)(2,1)S(1)}, bf16[224,512]{1,0:T(8,128)(2,1)S(1)}, u32[]{:S(2)}, u32[]{:S(2)}) collective-permute-start(bf16[224,512]{1,0:T(8,128)(2,1)S(1)} %get-tuple-element.245), channel_id=1, source_target_pairs={{0,4},{4,0},{8,12},{12,8},{1,5},{5,1},{9,13},{13,9},{2,6},{6,2},{1... | collective-permute-start | bytes 688136 | tf_op jit(solution)/shard_map/ppermute | solution.py:194
  176.7 15.4 %copy-start.10 = (bf16[8,2,128,256]{3,2,1,0:T(8,128)(2,1)S(1)}, bf16[8,2,128,256]{3,2,1,0:T(8,128)(2,1)}, u32[]{:S(2)}) copy-start(bf16[8,2,128,256]{3,2,1,0:T(8,128)(2,1)} %refs_2_.9) | copy-start | bytes 3145732
  177.9 16.3 %collective-permute-start.13 = (bf16[288,512]{1,0:T(8,128)(2,1)S(1)}, bf16[288,512]{1,0:T(8,128)(2,1)S(1)}, u32[]{:S(2)}, u32[]{:S(2)}) collective-permute-start(bf16[288,512]{1,0:T(8,128)(2,1)S(1)} %add.396), channel_id=1, source_target_pairs={{0,8},{4,12},{8,0},{12,4},{1,9},{5,13},{9,1},{13,5},{2,10},{6,14},... | collective-permute-start | bytes 884744 | tf_op jit(solution)/shard_map/ppermute | solution.py:194
  192.8 0.7 copy-start.14
  193.5 0.7 copy-start.17
  194.2 14.7 %collective-permute-start.16 = (bf16[224,512]{1,0:T(8,128)(2,1)S(1)}, bf16[224,512]{1,0:T(8,128)(2,1)S(1)}, u32[]{:S(2)}, u32[]{:S(2)}) collective-permute-start(bf16[224,512]{1,0:T(8,128)(2,1)S(1)} %get-tuple-element.250), channel_id=1, source_target_pairs={{0,8},{4,12},{8,0},{12,4},{1,9},{5,13},{9,1},{13,5},{2,10},{6,14},... | collective-permute-start | bytes 688136 | tf_op jit(solution)/shard_map/ppermute | solution.py:194
  197.1 1.2 copy-start.2
  200.4 3.2 %copy-start.18 = (bf16[224,512]{1,0:T(8,128)(2,1)S(1)}, bf16[224,512]{1,0:T(8,128)(2,1)}, u32[]{:S(2)}) copy-start(bf16[224,512]{1,0:T(8,128)(2,1)} %copy-done.17) | copy-start | bytes 688132
  203.5 2.5 %copy-start.11 = (bf16[8,2,128,256]{3,2,1,0:T(8,128)(2,1)S(1)}, bf16[8,2,128,256]{3,2,1,0:T(8,128)(2,1)}, u32[]{:S(2)}) copy-start(bf16[8,2,128,256]{3,2,1,0:T(8,128)(2,1)} %refs_2_.9) | copy-start | bytes 3145732
  203.5 2.5 %copy-start.19 = (u32[32]{0:T(128)S(1)}, u32[32]{0:T(128)}, u32[]{:S(2)}) copy-start(u32[32]{0:T(128)} %constant.209) | copy-start | bytes 388
  203.5 7.6 %collective-permute-start.17 = (bf16[224,512]{1,0:T(8,128)(2,1)S(1)}, bf16[224,512]{1,0:T(8,128)(2,1)S(1)}, u32[]{:S(2)}, u32[]{:S(2)}) collective-permute-start(bf16[224,512]{1,0:T(8,128)(2,1)S(1)} %get-tuple-element.258), channel_id=1, source_target_pairs={{0,4},{4,0},{8,12},{12,8},{1,5},{5,1},{9,13},{13,9},{2,6},{6,2},{1... | collective-permute-start | bytes 688136 | tf_op jit(solution)/shard_map/ppermute | solution.py:194
  206.0 0.9 copy-start.15
Sparse Core Ops, SparseCore 0:
  121.8 14.7 all-gather.8

commit v2 on v1

--- a/solution.py
+++ b/solution.py
@@ -212,7 +212,7 @@
     chunk = 64
     pooled = inst_count == 4
     if pooled:
-        own_cap, near_cap, far_cap, flex_cap = rows // 2, 448 * rows // 1024, 224 * rows // 1024, 288 * rows // 1024
+        own_cap, near_cap, far_cap, flex_cap = rows // 2, rows // 2, 224 * rows // 1024, 288 * rows // 1024
     else:
         own_cap = near_cap = far_cap = flex_cap = 0
     holder = ids // held

time: 222 us -> 226 us (1.018)
  waiting for transfers between devices: 17.8 us -> 21.6 us
  blocking collectives: 56.2 us -> 52.5 us
    ppermute x15, waiting for transfers between devices: 17.7 us -> 21.6 us  [swap(): return lax.ppermute(x, axis, [(i, i ^ distance) for i in range(count)])]
    all_gather x4, blocking collectives: 56.2 us -> 52.5 us  [gathered(): return lax.all_gather(part, 'tp', axis=0, tiled=False)]
    unnamed x40 -> x58, local copies, waits for them, and re-layouts: 9.72 us -> 9.48 us
  transfers between devices with their start and end apart: 18 -> 18, of which waited for: 6 -> 5; matrix products, arithmetic and copies ran while one was open for 7% -> 8% of each run, Pallas kernels for 29% -> 29%
where the time goes in v2:
time: 226 us; the launch traced here: 225 us
  Pallas kernels  71.8 us (32%)
  blocking collectives  52.5 us (23%)
  starting transfers between devices  31.2 us (14%)
  waiting for transfers between devices  21.6 us (10%)
  between operations  18.3 us (8%)
  local copies, waits for them, and re-layouts  17.6 us (8%)
  other arithmetic  7.47 us (3%)
  matrix products  4.75 us (2%)
    all_gather x4, blocking collectives, gathered(): return lax.all_gather(part, 'tp', axis=0, tiled=False)  52.5 us
    pallas_call x5, Pallas kernels, down(): pl.pallas_call(lambda *refs: down_kernel(len(xs), *refs), out_shape=jax.S...  34.5 us
    ppermute x15, starting transfers between devices, swap(): return lax.ppermute(x, axis, [(i, i ^ distance) for i in range(count)])  23.3 us
    ppermute x15, waiting for transfers between devices, swap(): return lax.ppermute(x, axis, [(i, i ^ distance) for i in range(count)])  21.6 us
    pallas_call x3, Pallas kernels, gather(): pl.pallas_call(lambda *refs: gather_kernel(starts, *refs), out_shape=[jax...  16.3 us
    pallas_call x1, Pallas kernels, base_blocks(): pl.pallas_call(base_kernel, out_shape=[jax.ShapeDtypeStruct((share, rows,...  12.3 us
    unnamed x58, local copies, waits for them, and re-layouts  9.48 us
    pallas_call x5, Pallas kernels, up(): pl.pallas_call(lambda *refs: up_kernel(len(parts), *refs), out_shape=[jax...  6.61 us
  transfers between devices with their start and end apart: 18, of which 5 were waited for; matrix products, arithmetic and copies ran while one was open for 8% of the time, Pallas kernels for 29%

profile of v2, /device:TPU:0, one launch (start us, length us, event | category | flops | bytes accessed | tf_op | source)
XLA Modules:
  0.0 225.3 jit_solution(5944934105800777293)
XLA Ops:
  6.5 0.7 copy.107
  7.4 0.3 fusion.10
  7.7 0.6 fusion.32
  9.6 0.8 select_reduce_fusion
  11.1 5.1 %collective-permute-start.4 = (s32[1,513]{1,0:T(1,128)S(1)}, s32[1,513]{1,0:T(1,128)S(1)}, u32[]{:S(2)}, u32[]{:S(2)}) collective-permute-start(s32[1,513]{1,0:T(1,128)S(1)} %pad_add_fusion.2), channel_id=1, source_target_pairs={{0,12},{4,8},{8,4},{12,0},{1,13},{5,9},{9,5},{13,1},{2,14},{6,10},... | collective-permute-start | bytes 6164 | tf_op jit(solution)/shard_map/ppermute | solution.py:194
  16.2 0.6 collective-permute-start.2
  16.9 0.7 copy.106
  17.8 2.9 %collective-permute-done.3 = s32[1,513]{1,0:T(1,128)S(1)} collective-permute-done((s32[1,513]{1,0:T(1,128)S(1)}, s32[1,513]{1,0:T(1,128)S(1)}, u32[]{:S(2)}, u32[]{:S(2)}) %collective-permute-start.3) | collective-permute-done | bytes 2084 | tf_op jit(solution)/shard_map/ppermute | solution.py:194
  20.7 5.1 %gather.7 = bf16[288,2048]{1,0:T(8,128)(2,1)} custom-call(s32[1,1024]{1,0:T(1,128)S(1)} %compare_select_fusion.7.refs_0_, bf16[1024,2048]{1,0:T(8,128)(2,1)} %bitcast.56), custom_call_target="tpu_custom_call" | custom-call | flops 1024 | bytes 1024 | tf_op jit(solution)/shard_map/gather/pallas_call | solution.py:23
  25.8 2.0 collective-permute-start.5
  27.8 3.1 %gather.8 = bf16[256,2048]{1,0:T(8,128)(2,1)} custom-call(s32[1,1024]{1,0:T(1,128)S(1)} %compare_select_fusion.7.refs_0_, bf16[1024,2048]{1,0:T(8,128)(2,1)S(1)} %bitcast.59), custom_call_target="tpu_custom_call" | custom-call | flops 1024 | bytes 1024 | tf_op jit(solution)/shard_map/gather/pallas_call | solution.py:23
  31.1 8.2 %gather.9 = (bf16[224,2048]{1,0:T(8,128)(2,1)S(1)}, bf16[512,2048]{1,0:T(8,128)(2,1)S(1)}, bf16[224,2048]{1,0:T(8,128)(2,1)S(1)}, bf16[256,2048]{1,0:T(8,128)(2,1)}) custom-call(s32[1,1024]{1,0:T(1,128)S(1)} %compare_select_fusion.7.refs_0_, bf16[1024,2048]{1,0:T(8,128)(2,1)} %bitcast.57), custom_call_target="tpu_custom_call" | custom-call | flops 1024 | bytes 1024 | tf_op jit(solution)/shard_map/gather/pallas_call | solution.py:23
  39.3 0.9 copy-done.3
  40.3 0.9 copy-done.4
  41.2 12.3 %base.1 = bf16[4,1024,512]{2,1,0:T(8,128)(2,1)S(1)} custom-call(s32[4]{0:T(128)S(1)} %iota.37.order_ref, bf16[1024,2048]{1,0:T(8,128)(2,1)S(1)} %bitcast.60, bf16[2048,2048]{1,0:T(8,128)(2,1)} %weight_ref.1), custom_call_target="tpu_custom_call" | custom-call | flops 1024 | bytes 1024 | tf_op jit(solution)/shard_map/base/pallas_call | solution.py:145
  53.5 2.0 copy-done.1
  55.5 0.5 slice.63
  56.0 0.5 slice.65
  56.5 0.6 slice.64
  59.2 2.9 %collective-permute-start.7 = (s32[]{:T(128)}, s32[]{:T(128)}, u32[]{:S(2)}, u32[]{:S(2)}) collective-permute-start(s32[]{:T(128)} %reduce_max.24), channel_id=1, source_target_pairs={{0,16},{16,0},{1,17},{17,1},{2,18},{18,2},{3,19},{19,3},{4,20},{20... | collective-permute-start | bytes 20 | tf_op jit(solution)/shard_map/ppermute | solution.py:297
  62.3 5.0 %all-to-all-start.1 = ((bf16[4,1024,512]{2,1,0:T(8,128)(2,1)}), bf16[4,1024,512]{2,1,0:T(8,128)(2,1)}, u32[]{:S(2)}, u32[]{:S(2)}) async-start(bf16[4,1024,512]{2,1,0:T(8,128)(2,1)} %copy-done.1), calls=%async_computation.1 | async-start | bytes 8388608 | tf_op jit(solution)/shard_map/all_to_all | solution.py:290
  67.8 0.7 pad_add_fusion.4
  69.1 10.2 %collective-permute-done.6.refs_3_ = bf16[256,2048]{1,0:T(8,128)(2,1)} collective-permute-done((bf16[256,2048]{1,0:T(8,128)(2,1)}, bf16[256,2048]{1,0:T(8,128)(2,1)}, u32[]{:S(2)}, u32[]{:S(2)}) %collective-permute-start.6) | collective-permute-done | bytes 1048608 | tf_op jit(solution)/shard_map/ppermute | solution.py:194
  79.3 1.0 collective-permute-start.8
  80.3 6.1 %down.9 = bf16[288,256]{1,0:T(8,128)(2,1)S(1)} custom-call(s32[8]{0:T(128)S(1)} %copy-done.21, s32[288,1]{1,0:T(8,128)S(1)} %slice.79.refs_1_.refs_0_, bf16[288,2048]{1,0:T(8,128)(2,1)} %collective-permute-done.5.refs_2_, bf16[8,2048,256]{2,1,0:T(8,128)(2,1)} %refs_4_.3), custom_call_target="tpu_custom_call" | custom-call | flops 1024 | bytes 1024 | tf_op jit(solution)/shard_map/down/pallas_call | solution.py:70
  86.4 7.8 %down.10 = bf16[512,256]{1,0:T(8,128)(2,1)} custom-call(s32[8]{0:T(128)S(1)} %copy-done.21, s32[512,1]{1,0:T(8,128)S(1)} %and_select_fusion.3.refs_1_.refs_0_, bf16[512,2048]{1,0:T(8,128)(2,1)S(1)} %get-tuple-element.224.refs_2_, bf16[8,2048,256]{2,1,0:T(8,128)(2,1)} %refs_4_.3), custom_call_target="tpu_custom_call" | custom-call | flops 1024 | bytes 1024 | tf_op jit(solution)/shard_map/down/pallas_call | solution.py:70
  94.3 25.2 %all-gather.1 = bf16[1152,256]{1,0:T(8,128)(2,1)S(1)} all-gather(bf16[288,256]{1,0:T(8,128)(2,1)S(1)} %down.9), channel_id=3, replica_groups=mesh['groups'=2,'inst'=4,'tp'=4] {'tp'}, dimensions={0}, use_global_device_ids=true | all-gather | bytes 737280 | tf_op jit(solution)/shard_map/all_gather | solution.py:270
  119.4 1.8 up.9
  121.2 2.1 collective-permute-start.10
  123.3 1.1 copy.104
  124.4 1.0 copy.94
  125.6 1.0 collective-permute-start.9
  126.6 7.6 %down.11 = bf16[480,256]{1,0:T(8,128)(2,1)S(1)} custom-call(s32[8]{0:T(128)S(1)} %copy-done.21, s32[480,1]{1,0:T(8,128)S(1)} %copy.91.refs_1_.refs_0_, bf16[224,2048]{1,0:T(8,128)(2,1)} %collective-permute-done.8.refs_2_, bf16[256,2048]{1,0:T(8,128)(2,1)} %collective-permute-done.6.refs_3_, bf16[8,2048,256]{2,1,0:T(8,128)(2,1)} %refs_4_.3), custom_call_target="tpu_custom_call" | custom-call | flops 1024 | bytes 1024 | tf_op jit(solution)/shard_map/down/pallas_call | solution.py:70
  134.1 9.3 %all-gather.2 = bf16[1920,256]{1,0:T(8,128)(2,1)S(1)} all-gather(bf16[480,256]{1,0:T(8,128)(2,1)S(1)} %down.11), channel_id=4, replica_groups=mesh['groups'=2,'inst'=4,'tp'=4] {'tp'}, dimensions={0}, use_global_device_ids=true | all-gather | bytes 1228800 | tf_op jit(solution)/shard_map/all_gather | solution.py:270
  143.5 0.8 up.10
  144.3 0.7 copy-done.5
  144.9 6.1 %down.12 = bf16[288,256]{1,0:T(8,128)(2,1)S(1)} custom-call(s32[8]{0:T(128)S(1)} %copy-done.21, s32[288,1]{1,0:T(8,128)S(1)} %slice.81.refs_1_.refs_0_, bf16[288,2048]{1,0:T(8,128)(2,1)} %collective-permute-done.11.refs_2_, bf16[8,2048,256]{2,1,0:T(8,128)(2,1)} %refs_4_.3), custom_call_target="tpu_custom_call" | custom-call | flops 1024 | bytes 1024 | tf_op jit(solution)/shard_map/down/pallas_call | solution.py:70
  151.1 8.0 %all-gather.3 = bf16[1152,256]{1,0:T(8,128)(2,1)S(1)} all-gather(bf16[288,256]{1,0:T(8,128)(2,1)S(1)} %down.12), channel_id=5, replica_groups=mesh['groups'=2,'inst'=4,'tp'=4] {'tp'}, dimensions={0}, use_global_device_ids=true | all-gather | bytes 737280 | tf_op jit(solution)/shard_map/all_gather | solution.py:270
  159.0 1.3 up.11
  160.6 0.7 select_select_fusion.refs_1_
  161.3 0.8 copy.105
  162.0 0.6 iota_add_fusion.1
  162.6 0.8 copy.93.refs_1_.refs_0_
  163.4 1.8 collective-permute-start.15
  165.3 3.8 %collective-permute-start.14 = (bf16[224,512]{1,0:T(8,128)(2,1)}, bf16[224,512]{1,0:T(8,128)(2,1)S(1)}, u32[]{:S(2)}, u32[]{:S(2)}) collective-permute-start(bf16[224,512]{1,0:T(8,128)(2,1)} %copy-done.5), channel_id=1, source_target_pairs={{0,12},{4,8},{8,4},{12,0},{1,13},{5,9},{9,5},{13,1},{2,14},{6,10},... | collective-permute-start | bytes 688136 | tf_op jit(solution)/shard_map/ppermute | solution.py:194
  169.1 0.6 collective-permute-done.10.refs_3_
  169.7 6.9 %down.13 = bf16[480,256]{1,0:T(8,128)(2,1)S(1)} custom-call(s32[8]{0:T(128)} %refs_0_.9, s32[480,1]{1,0:T(8,128)S(1)} %copy.93.refs_1_.refs_0_, bf16[224,2048]{1,0:T(8,128)(2,1)S(1)} %collective-permute-done.9.refs_2_, bf16[256,2048]{1,0:T(8,128)(2,1)S(1)} %collective-permute-done.10.refs_3_, bf16[8,2048,256]{2,1,0:T(8,128)(2,1)} %refs_4_.3), custom_call_target="tpu_custom_call" | custom-call | flops 1024 | bytes 1024 | tf_op jit(solution)/shard_map/down/pallas_call | solution.py:70
  176.7 1.1 add.379
  177.8 2.1 collective-permute-start.13
  179.9 10.0 %all-gather.4 = bf16[1920,256]{1,0:T(8,128)(2,1)S(1)} all-gather(bf16[480,256]{1,0:T(8,128)(2,1)S(1)} %down.13), channel_id=6, replica_groups=mesh['groups'=2,'inst'=4,'tp'=4] {'tp'}, dimensions={0}, use_global_device_ids=true | all-gather | bytes 1228800 | tf_op jit(solution)/shard_map/all_gather | solution.py:270
  189.9 0.8 up.12
  190.7 0.7 copy-done.19
  191.3 0.7 copy-done.26
  192.0 5.3 %collective-permute-done.13.refs_3_ = bf16[288,512]{1,0:T(8,128)(2,1)S(1)} collective-permute-done((bf16[288,512]{1,0:T(8,128)(2,1)S(1)}, bf16[288,512]{1,0:T(8,128)(2,1)S(1)}, u32[]{:S(2)}, u32[]{:S(2)}) %collective-permute-start.13) | collective-permute-done | bytes 294944 | tf_op jit(solution)/shard_map/ppermute | solution.py:194
  197.4 1.2 copy-done.2
  198.6 2.0 up.13
  200.7 3.0 %convert_reduce_fusion = f32[1024,512]{1,0:T(8,128)S(1)} fusion(bf16[4,1024,512]{2,1,0:T(8,128)(2,1)} %all-to-all-done.1), kind=kLoop, calls=%fused_computation.13 | loop fusion | flops 3670016 | bytes 6291456 | tf_op jit(solution)/shard_map/reduce_sum | solution.py:392
  203.8 3.5 %collective-permute-start.17 = (bf16[256,512]{1,0:T(8,128)(2,1)S(1)}, bf16[256,512]{1,0:T(8,128)(2,1)S(1)}, u32[]{:S(2)}, u32[]{:S(2)}) collective-permute-start(bf16[256,512]{1,0:T(8,128)(2,1)S(1)} %get-tuple-element.258), channel_id=1, source_target_pairs={{0,4},{4,0},{8,12},{12,8},{1,5},{5,1},{9,13},{13,9},{2,6},{6,2},{1... | collective-permute-start | bytes 786440 | tf_op jit(solution)/shard_map/ppermute | solution.py:194
  207.3 2.4 %fusion.6 = f32[1024,512]{1,0:T(8,128)} fusion(f32[1024,512]{1,0:T(8,128)S(1)} %convert_reduce_fusion, s32[1024]{0:T(1024)S(1)} %copy-done.24, bf16[256,512]{1,0:T(8,128)(2,1)S(1)} %copy-done.27, bf16[512,512]{1,0:T(8,128)(2,1)S(1)} %up.13), kind=kOutput, calls=%fused_computation.20 | convolution fusion | flops 808189952 | bytes 4984832 | tf_op jit(solution)/shard_map/dot_general | solution.py:258
  209.7 0.9 copy-done.20
  210.6 2.1 convolution_add_fusion.1.refs_0_
  212.7 2.6 %collective-permute-done.17.refs_4_ = bf16[256,512]{1,0:T(8,128)(2,1)S(1)} collective-permute-done((bf16[256,512]{1,0:T(8,128)(2,1)S(1)}, bf16[256,512]{1,0:T(8,128)(2,1)S(1)}, u32[]{:S(2)}, u32[]{:S(2)}) %collective-permute-start.17) | collective-permute-done | bytes 262176 | tf_op jit(solution)/shard_map/ppermute | solution.py:194
  215.3 2.0 finish.1
  217.4 1.1 reshape.627
  (102 shorter events, 2.1 us)
Async XLA Ops:
  9.5 0.8 copy-start.23
  11.1 6.7 %collective-permute-start.4 = (s32[1,513]{1,0:T(1,128)S(1)}, s32[1,513]{1,0:T(1,128)S(1)}, u32[]{:S(2)}, u32[]{:S(2)}) collective-permute-start(s32[1,513]{1,0:T(1,128)S(1)} %pad_add_fusion.2), channel_id=1, source_target_pairs={{0,12},{4,8},{8,4},{12,0},{1,13},{5,9},{9,5},{13,1},{2,14},{6,10},... | collective-permute-start | bytes 6164 | tf_op jit(solution)/shard_map/ppermute | solution.py:194
  16.2 4.5 %collective-permute-start.3 = (s32[1,513]{1,0:T(1,128)S(1)}, s32[1,513]{1,0:T(1,128)S(1)}, u32[]{:S(2)}, u32[]{:S(2)}) collective-permute-start(s32[1,513]{1,0:T(1,128)S(1)} %pad_add_fusion.1), channel_id=1, source_target_pairs={{0,8},{4,12},{8,0},{12,4},{1,9},{5,13},{9,1},{13,5},{2,10},{6,14},... | collective-permute-start | bytes 6164 | tf_op jit(solution)/shard_map/ppermute | solution.py:194
  16.2 4.5 %collective-permute-start.2 = (s32[1,513]{1,0:T(1,128)S(1)}, s32[1,513]{1,0:T(1,128)S(1)}, u32[]{:S(2)}, u32[]{:S(2)}) collective-permute-start(s32[1,513]{1,0:T(1,128)S(1)} %pad_add_fusion), channel_id=1, source_target_pairs={{0,4},{4,0},{8,12},{12,8},{1,5},{5,1},{9,13},{13,9},{2,6},{6,2},{1... | collective-permute-start | bytes 6164 | tf_op jit(solution)/shard_map/ppermute | solution.py:194
  17.6 106.8 %copy-start.17 = (s32[1,1,4,256]{3,1,2,0:T(1,128)}, s32[1,1,4,256]{3,1,2,0:T(1,128)S(1)}, u32[]{:S(2)}) copy-start(s32[1,1,4,256]{3,1,2,0:T(1,128)S(1)} %copy.106) | copy-start | bytes 12292
  17.8 13.3 %copy-start.15 = (s32[1,1024]{1,0:T(1,128)}, s32[1,1024]{1,0:T(1,128)S(1)}, u32[]{:S(2)}) copy-start(s32[1,1024]{1,0:T(1,128)S(1)} %compare_select_fusion.7.refs_0_) | copy-start | bytes 12292
  20.7 7.1 %copy-start.6 = (bf16[4,256,2048]{2,1,0:T(8,128)(2,1)S(1)}, bf16[4,256,2048]{2,1,0:T(8,128)(2,1)}, u32[]{:S(2)}) copy-start(bf16[4,256,2048]{2,1,0:T(8,128)(2,1)} %param.8) | copy-start | bytes 12582916
  25.8 53.5 %collective-permute-start.5 = (bf16[288,2048]{1,0:T(8,128)(2,1)}, bf16[288,2048]{1,0:T(8,128)(2,1)}, u32[]{:S(2)}, u32[]{:S(2)}) collective-permute-start(bf16[288,2048]{1,0:T(8,128)(2,1)} %gather.7), channel_id=1, source_target_pairs={{0,8},{4,12},{8,0},{12,4},{1,9},{5,13},{9,1},{13,5},{2,10},{6,14},... | collective-permute-start | bytes 3538952 | tf_op jit(solution)/shard_map/ppermute | solution.py:194
  30.9 48.4 %collective-permute-start.6 = (bf16[256,2048]{1,0:T(8,128)(2,1)}, bf16[256,2048]{1,0:T(8,128)(2,1)}, u32[]{:S(2)}, u32[]{:S(2)}) collective-permute-start(bf16[256,2048]{1,0:T(8,128)(2,1)} %gather.8), channel_id=1, source_target_pairs={{0,4},{4,0},{8,12},{12,8},{1,5},{5,1},{9,13},{13,9},{2,6},{6,2},{1... | collective-permute-start | bytes 3145736 | tf_op jit(solution)/shard_map/ppermute | solution.py:194
  31.1 25.4 %copy-start.13 = (s32[512,1]{1,0:T(8,128)}, s32[512,1]{1,0:T(8,128)S(1)}, u32[]{:S(2)}) copy-start(s32[512,1]{1,0:T(8,128)S(1)} %and_select_fusion.2) | copy-start | bytes 6148
  31.1 10.1 %copy-start.7 = (bf16[4,256,2048]{2,1,0:T(8,128)(2,1)S(1)}, bf16[4,256,2048]{2,1,0:T(8,128)(2,1)}, u32[]{:S(2)}) copy-start(bf16[4,256,2048]{2,1,0:T(8,128)(2,1)} %param.8) | copy-start | bytes 12582916
  39.3 0.9 copy-start.3
  40.2 0.9 copy-start.4
  53.5 2.0 copy-start.1
  59.2 9.3 %collective-permute-start.7 = (s32[]{:T(128)}, s32[]{:T(128)}, u32[]{:S(2)}, u32[]{:S(2)}) collective-permute-start(s32[]{:T(128)} %reduce_max.24), channel_id=1, source_target_pairs={{0,16},{16,0},{1,17},{17,1},{2,18},{18,2},{3,19},{19,3},{4,20},{20... | collective-permute-start | bytes 20 | tf_op jit(solution)/shard_map/ppermute | solution.py:297
  62.2 5.2 %slice-start = ((s32[512,1]{1,0:T(8,128)}), s32[224,1]{1,0:T(8,128)S(1)}, s32[]{:S(2)}) async-start(s32[512,1]{1,0:T(8,128)} %copy-done.13), calls=%async_computation.4 | async-start | bytes 229376 | tf_op jit(solution)/shard_map/slice | solution.py:345
  62.2 18.1 %copy-start.21 = (s32[8]{0:T(128)S(1)}, s32[8]{0:T(128)}, u32[]{:S(2)}) copy-start(s32[8]{0:T(128)} %refs_0_.9) | copy-start | bytes 100
  62.3 135.1 %all-to-all-start.1 = ((bf16[4,1024,512]{2,1,0:T(8,128)(2,1)}), bf16[4,1024,512]{2,1,0:T(8,128)(2,1)}, u32[]{:S(2)}, u32[]{:S(2)}) async-start(bf16[4,1024,512]{2,1,0:T(8,128)(2,1)} %copy-done.1), calls=%async_computation.1 | async-start | bytes 8388608 | tf_op jit(solution)/shard_map/all_to_all | solution.py:290
  67.3 130.1 %all-gather.9.cloned.1.call-start = ((), (), s32[]{:S(2)}) async-start(), calls=%async_computation.2 | async-start | bytes 1310720 | tf_op jit(solution)/shard_map/all_gather | solution.py:270
  79.3 41.9 %collective-permute-start.8 = (bf16[224,2048]{1,0:T(8,128)(2,1)}, bf16[224,2048]{1,0:T(8,128)(2,1)}, u32[]{:S(2)}, u32[]{:S(2)}) collective-permute-start(bf16[224,2048]{1,0:T(8,128)(2,1)} %copy-done.4), channel_id=1, source_target_pairs={{0,12},{4,8},{8,4},{12,0},{1,13},{5,9},{9,5},{13,1},{2,14},{6,10},... | collective-permute-start | bytes 2752520 | tf_op jit(solution)/shard_map/ppermute | solution.py:194
  80.3 64.6 %collective-permute-start.11 = (bf16[288,2048]{1,0:T(8,128)(2,1)}, bf16[288,2048]{1,0:T(8,128)(2,1)}, u32[]{:S(2)}, u32[]{:S(2)}) collective-permute-start(bf16[288,2048]{1,0:T(8,128)(2,1)} %collective-permute-done.5.refs_2_), channel_id=1, source_target_pairs={{0,4},{4,0},{8,12},{12,8},{1,5},{5,1},{9,13},{13,9},{2,6},{6,2},{1... | collective-permute-start | bytes 3538952 | tf_op jit(solution)/shard_map/ppermute | solution.py:194
  121.2 48.5 %collective-permute-start.10 = (bf16[256,2048]{1,0:T(8,128)(2,1)}, bf16[256,2048]{1,0:T(8,128)(2,1)S(1)}, u32[]{:S(2)}, u32[]{:S(2)}) collective-permute-start(bf16[256,2048]{1,0:T(8,128)(2,1)} %get-tuple-element.228), channel_id=1, source_target_pairs={{0,4},{4,0},{8,12},{12,8},{1,5},{5,1},{9,13},{13,9},{2,6},{6,2},{1... | collective-permute-start | bytes 3145736 | tf_op jit(solution)/shard_map/ppermute | solution.py:194
  125.6 17.9 %copy-start.8 = (bf16[8,2,128,256]{3,2,1,0:T(8,128)(2,1)S(1)}, bf16[8,2,128,256]{3,2,1,0:T(8,128)(2,1)}, u32[]{:S(2)}) copy-start(bf16[8,2,128,256]{3,2,1,0:T(8,128)(2,1)} %refs_2_.9) | copy-start | bytes 3145732
  125.6 43.5 %collective-permute-start.9 = (bf16[224,2048]{1,0:T(8,128)(2,1)}, bf16[224,2048]{1,0:T(8,128)(2,1)S(1)}, u32[]{:S(2)}, u32[]{:S(2)}) collective-permute-start(bf16[224,2048]{1,0:T(8,128)(2,1)} %copy-done.3), channel_id=1, source_target_pairs={{0,8},{4,12},{8,0},{12,4},{1,9},{5,13},{9,1},{13,5},{2,10},{6,14},... | collective-permute-start | bytes 2752520 | tf_op jit(solution)/shard_map/ppermute | solution.py:194
  144.3 0.7 copy-start.5
  151.0 9.5 %copy-start.11 = (s32[1024,1]{1,0:T(8,128)S(1)}, s32[1024,1]{1,0:T(8,128)}, u32[]{:S(2)}) copy-start(s32[1024,1]{1,0:T(8,128)} %copy.104) | copy-start | bytes 12292
  151.0 9.5 %copy-start.12 = (s32[1024,1]{1,0:T(8,128)S(1)}, s32[1024,1]{1,0:T(8,128)}, u32[]{:S(2)}) copy-start(s32[1024,1]{1,0:T(8,128)} %copy.94) | copy-start | bytes 12292
  160.3 16.4 %collective-permute-start.12 = (bf16[288,512]{1,0:T(8,128)(2,1)}, bf16[288,512]{1,0:T(8,128)(2,1)}, u32[]{:S(2)}, u32[]{:S(2)}) collective-permute-start(bf16[288,512]{1,0:T(8,128)(2,1)} %up.11), channel_id=1, source_target_pairs={{0,4},{4,0},{8,12},{12,8},{1,5},{5,1},{9,13},{13,9},{2,6},{6,2},{1... | collective-permute-start | bytes 884744 | tf_op jit(solution)/shard_map/ppermute | solution.py:194
  163.4 27.2 %collective-permute-start.15 = (bf16[256,512]{1,0:T(8,128)(2,1)S(1)}, bf16[256,512]{1,0:T(8,128)(2,1)S(1)}, u32[]{:S(2)}, u32[]{:S(2)}) collective-permute-start(bf16[256,512]{1,0:T(8,128)(2,1)S(1)} %get-tuple-element.245), channel_id=1, source_target_pairs={{0,4},{4,0},{8,12},{12,8},{1,5},{5,1},{9,13},{13,9},{2,6},{6,2},{1... | collective-permute-start | bytes 786440 | tf_op jit(solution)/shard_map/ppermute | solution.py:194
  165.3 25.4 %collective-permute-start.14 = (bf16[224,512]{1,0:T(8,128)(2,1)}, bf16[224,512]{1,0:T(8,128)(2,1)S(1)}, u32[]{:S(2)}, u32[]{:S(2)}) collective-permute-start(bf16[224,512]{1,0:T(8,128)(2,1)} %copy-done.5), channel_id=1, source_target_pairs={{0,12},{4,8},{8,4},{12,0},{1,13},{5,9},{9,5},{13,1},{2,14},{6,10},... | collective-permute-start | bytes 688136 | tf_op jit(solution)/shard_map/ppermute | solution.py:194
  176.7 13.2 %copy-start.9 = (bf16[8,2,128,256]{3,2,1,0:T(8,128)(2,1)S(1)}, bf16[8,2,128,256]{3,2,1,0:T(8,128)(2,1)}, u32[]{:S(2)}) copy-start(bf16[8,2,128,256]{3,2,1,0:T(8,128)(2,1)} %refs_2_.9) | copy-start | bytes 3145732
  177.8 19.5 %collective-permute-start.13 = (bf16[288,512]{1,0:T(8,128)(2,1)S(1)}, bf16[288,512]{1,0:T(8,128)(2,1)S(1)}, u32[]{:S(2)}, u32[]{:S(2)}) collective-permute-start(bf16[288,512]{1,0:T(8,128)(2,1)S(1)} %add.379), channel_id=1, source_target_pairs={{0,8},{4,12},{8,0},{12,4},{1,9},{5,13},{9,1},{13,5},{2,10},{6,14},... | collective-permute-start | bytes 884744 | tf_op jit(solution)/shard_map/ppermute | solution.py:194
  190.6 0.7 copy-start.19
  191.3 0.7 copy-start.26
  197.3 15.4 %collective-permute-start.16 = (bf16[224,512]{1,0:T(8,128)(2,1)S(1)}, bf16[224,512]{1,0:T(8,128)(2,1)S(1)}, u32[]{:S(2)}, u32[]{:S(2)}) collective-permute-start(bf16[224,512]{1,0:T(8,128)(2,1)S(1)} %get-tuple-element.250), channel_id=1, source_target_pairs={{0,8},{4,12},{8,0},{12,4},{1,9},{5,13},{9,1},{13,5},{2,10},{6,14},... | collective-permute-start | bytes 688136 | tf_op jit(solution)/shard_map/ppermute | solution.py:194
  197.4 1.2 copy-start.2
  200.6 6.7 %copy-start.24 = (s32[1024]{0:T(1024)S(1)}, s32[1024]{0:T(1024)}, u32[]{:S(2)}) copy-start(s32[1024]{0:T(1024)} %copy-done.23) | copy-start | bytes 12292
  200.6 6.7 %copy-start.27 = (bf16[256,512]{1,0:T(8,128)(2,1)S(1)}, bf16[256,512]{1,0:T(8,128)(2,1)}, u32[]{:S(2)}) copy-start(bf16[256,512]{1,0:T(8,128)(2,1)} %copy-done.26) | copy-start | bytes 786436
  203.7 6.0 %copy-start.10 = (bf16[8,2,128,256]{3,2,1,0:T(8,128)(2,1)S(1)}, bf16[8,2,128,256]{3,2,1,0:T(8,128)(2,1)}, u32[]{:S(2)}) copy-start(bf16[8,2,128,256]{3,2,1,0:T(8,128)(2,1)} %refs_2_.9) | copy-start | bytes 3145732
  203.7 5.9 %copy-start.14 = (s32[1024,1]{0,1:T(1,128)S(1)}, s32[1024,1]{0,1:T(1,128)}, u32[]{:S(2)}) copy-start(s32[1024,1]{0,1:T(1,128)} %copy.105) | copy-start | bytes 12292
  203.7 5.9 %copy-start.16 = (s32[1,1024]{1,0:T(1,128)S(1)}, s32[1,1024]{1,0:T(1,128)}, u32[]{:S(2)}) copy-start(s32[1,1024]{1,0:T(1,128)} %copy-done.15) | copy-start | bytes 12292
  203.7 5.9 %copy-start.18 = (s32[1,1,4,256]{3,1,2,0:T(1,128)S(1)}, s32[1,1,4,256]{3,1,2,0:T(1,128)}, u32[]{:S(2)}) copy-start(s32[1,1,4,256]{3,1,2,0:T(1,128)} %copy-done.17) | copy-start | bytes 12292
  203.7 5.9 %copy-start.22 = (s32[8]{0:T(128)S(1)}, s32[8]{0:T(128)}, u32[]{:S(2)}) copy-start(s32[8]{0:T(128)} %refs_0_.9) | copy-start | bytes 100
  203.8 5.9 %copy-start.28 = (u32[32]{0:T(128)S(1)}, u32[32]{0:T(128)}, u32[]{:S(2)}) copy-start(u32[32]{0:T(128)} %constant.204) | copy-start | bytes 388
  203.8 11.6 %collective-permute-start.17 = (bf16[256,512]{1,0:T(8,128)(2,1)S(1)}, bf16[256,512]{1,0:T(8,128)(2,1)S(1)}, u32[]{:S(2)}, u32[]{:S(2)}) collective-permute-start(bf16[256,512]{1,0:T(8,128)(2,1)S(1)} %get-tuple-element.258), channel_id=1, source_target_pairs={{0,4},{4,0},{8,12},{12,8},{1,5},{5,1},{9,13},{13,9},{2,6},{6,2},{1... | collective-permute-start | bytes 786440 | tf_op jit(solution)/shard_map/ppermute | solution.py:194
  209.7 0.9 copy-start.20
  209.7 0.9 copy-start.25
Sparse Core Ops, SparseCore 0:
  121.4 14.8 all-gather.8
